TPU v7x, 256 devices: a whole 4x4x8 slice. The times are simulated.
256 devices in a mesh: ctx: 64 (over z, y, core), ch: 4 (over x).
Axes of the slice: x: 4, y: 4, z: 8, core: 2. Of those that a mesh axis runs over, the one named last changes fastest.
Arguments:
- query_branch: bfloat16 [16384, 2048], P('ctx', 'ch'), may hold values from -6 to 6
- key_branch: bfloat16 [16384, 2048], P('ctx', 'ch'), may hold values from -6 to 6
- value_branch: bfloat16 [16384, 2048], P('ctx', 'ch'), may hold values from -6 to 6
- grad_output: bfloat16 [16384, 2048], P('ctx', 'ch'), may hold values from -6 to 6
- conv_output: bfloat16 [16384, 2048], P('ctx', 'ch'), may hold values from -6 to 6
- filters: float32 [16384, 512], P('ctx'), may hold values from -0.0625 to 0.0625
- genome_blocks: int32 [8], replicated, may hold values from 1 to 32, 64 in all
Outputs:
- grad_query: bfloat16 [16384, 2048], P('ctx', 'ch')
- grad_key: bfloat16 [16384, 2048], P('ctx', 'ch')
- grad_value: bfloat16 [16384, 2048], P('ctx', 'ch')
- grad_filters: float32 [16384, 512], P('ctx', 'ch')
Inputs may be any that keep to these rules, and one draw needn't show every extreme that they name: `genome_blocks`: the genomes lie in order and fill the row; the longest covers exactly 32 shards.
All inputs are finite; a program needn't handle non-finite values.
Results may differ from a plain program's by a relative error of at most 0.001.
Values sent between devices are 32-bit elements; how exact they have to be, the bound alone decides.
No kernel may reach another device: no remote copies, remote signals or barrier semaphores. Data moves between devices by JAX's collectives and lax.ppermute only.
A program may use at most 128 MiB of HBM per device.

v0:
```python
import functools

import jax
import jax.numpy as jnp
import ml_dtypes
import numpy as np
from jax import lax
from jax.experimental import pallas as pl
from jax.experimental.pallas import tpu as pltpu
from jax.sharding import PartitionSpec as P

BLOCK = 256
LANES = 128
OWN = 8
PLANES = 4
NCTX = 64
MOST = 32
GENOMES = 8
UNROLL = 4
IN_ROWS = 36
OUT_ROWS = 20
F32 = jnp.float32
BF16 = jnp.bfloat16


def split_table(table):
    high = table.astype(ml_dtypes.bfloat16)
    low = (table - high.astype(np.float64)).astype(ml_dtypes.bfloat16)
    return high, low


def dft_tables():
    freq = np.arange(BLOCK)
    sample = np.arange(BLOCK)
    phase = (sample[:, None] * (2 * freq[None, :] + 1)) % (4 * BLOCK)
    angle = phase * (np.pi / (2 * BLOCK))
    forward = np.concatenate([np.cos(angle), -np.sin(angle)], axis=1)
    inverse = forward.T / BLOCK
    return split_table(forward) + split_table(inverse)


def dot3(x, high, low):
    x_high = x.astype(BF16)
    x_low = (x - x_high.astype(F32)).astype(BF16)
    total = jnp.dot(x_low, high, preferred_element_type=F32)
    total = total + jnp.dot(x_high, low, preferred_element_type=F32)
    return total + jnp.dot(x_high, high, preferred_element_type=F32)


def pack_kernel(q_ref, k_ref, v_ref, g_ref, f_ref, out_ref, turned):
    for which, (a_ref, b_ref) in enumerate(((q_ref, k_ref), (g_ref, v_ref))):
        product = a_ref[...].astype(F32) * b_ref[...].astype(F32)
        for half in range(2):
            turned[half] = product[half * LANES : (half + 1) * LANES, :].T
        for half in range(2):
            for quarter in range(PLANES):
                for r in range(2):
                    rows = turned[half, pl.ds(LANES * quarter + r, NCTX, stride=2), :]
                    first = 16 * which + 8 * half + 2 * quarter + r
                    out_ref[pl.ds(first, NCTX, stride=IN_ROWS), :] = rows
    for half in range(2):
        turned[half, 0:LANES, :] = f_ref[half * LANES : (half + 1) * LANES, :].T
        for r in range(2):
            rows = turned[half, pl.ds(r, NCTX, stride=2), :]
            out_ref[pl.ds(32 + 2 * half + r, NCTX, stride=IN_ROWS), :] = rows


def signs():
    lane = lax.broadcasted_iota(jnp.int32, (1, BLOCK), 1)
    return (1 - 2 * (lane % 2)).astype(F32)


def load4(ref, row):
    return [ref[pl.ds(row, OWN), pl.ds(LANES * i, LANES)] for i in range(4)]


def store4(ref, row, values):
    for i in range(4):
        ref[pl.ds(row, OWN), pl.ds(LANES * i, LANES)] = values[i]


def add_conj(total, first, second):
    out = list(total)
    for i in range(2):
        a_re, a_im, b_re, b_im = first[i], first[i + 2], second[i], second[i + 2]
        out[i] = out[i] + (a_re * b_re + a_im * b_im)
        out[i + 2] = out[i + 2] + (a_re * b_im - a_im * b_re)
    return tuple(out)


def sweep(first_ref, first_row, second_ref, second_row, count, start):
    def step(c, total):
        for u in range(UNROLL):
            a = load4(first_ref, pl.multiple_of(OWN * (first_row + UNROLL * c + u), OWN))
            b = load4(second_ref, pl.multiple_of(OWN * (second_row + UNROLL * c + u), OWN))
            total = add_conj(total, a, b)
        return total

    return lax.fori_loop(0, (count + UNROLL - 1) // UNROLL, step, start)


def lag_kernel(
    genome_ref, plane_ref, x_ref, fh_ref, fl_ref, ih_ref, il_ref,
    lag_ref, carried_ref, gated, lags, flat, place,
):
    def mark(g, begin):
        count = genome_ref[g]

        def one(b, _):
            place[begin + b] = begin + b + UNROLL * g
            return 0

        lax.fori_loop(0, count, one, 0)
        return begin + count

    lax.fori_loop(0, GENOMES, mark, jnp.int32(0))
    carried_ref[...] = jnp.zeros_like(carried_ref)
    lags[...] = jnp.zeros_like(lags)
    gated[OWN * NCTX :, :] = jnp.zeros((OWN * UNROLL, 2 * BLOCK), F32)
    group = 16
    for part in range(NCTX // group):
        for which in range(2):
            rows = []
            for s in range(part * group, (part + 1) * group):
                base = IN_ROWS * s + 16 * which
                rows.append(
                    jnp.concatenate([x_ref[base : base + 8, :], x_ref[base + 8 : base + 16, :]], 1)
                )
            spec = dot3(jnp.concatenate(rows, 0), fh_ref[...], fl_ref[...])
            if which == 0:
                gated[OWN * group * part : OWN * group * (part + 1), :] = spec
            else:
                for i in range(group):
                    row = pl.multiple_of(OWN * place[part * group + i], OWN)
                    carried_ref[pl.ds(row, OWN), :] = spec[OWN * i : OWN * (i + 1), :]

    def genome(g, begin):
        count = genome_ref[g]

        def one_lag(d, _):
            row = pl.multiple_of(OWN * d, OWN)
            start = tuple(load4(lags, row))
            store4(
                lags,
                row,
                sweep(gated, begin, carried_ref, begin + UNROLL * g + d, count - d, start),
            )
            return 0

        lax.fori_loop(0, count, one_lag, 0)
        return begin + count

    lax.fori_loop(0, GENOMES, genome, jnp.int32(0))
    sign = signs()
    here, after = lags[: OWN * MOST, :], lags[OWN : OWN * (MOST + 1), :]
    spec = jnp.concatenate(
        [here[:, :BLOCK] + sign * after[:, BLOCK:], here[:, BLOCK:] - sign * after[:, :BLOCK]], 1
    )
    rows = dot3(spec, ih_ref[...], il_ref[...])
    for half in range(2):
        flat[half] = rows[:, half * LANES : (half + 1) * LANES]
    for quarter in range(PLANES):
        slot = lax.rem(quarter + PLANES - plane_ref[0], PLANES)
        for half in range(2):
            for r in range(2):
                rows = flat[half, pl.ds(2 * quarter + r, MOST, stride=OWN), :]
                lag_ref[slot, pl.ds(2 * half + r, MOST, stride=4), :] = rows


def back_kernel(
    genome_ref, plane_ref, carried_ref, f0_ref, f1_ref, f2_ref, f3_ref,
    fh_ref, fl_ref, ih_ref, il_ref, out_ref, filt, back, flat,
):
    for k, f_ref in enumerate((f0_ref, f1_ref, f2_ref, f3_ref)):
        quarter = lax.rem(plane_ref[0] + PLANES - k, PLANES)
        for half in range(2):
            for r in range(2):
                rows = f_ref[pl.ds(2 * half + r, MOST, stride=4), :]
                flat[half, pl.ds(2 * quarter + r, MOST, stride=OWN), :] = rows
    spec = dot3(jnp.concatenate([flat[0], flat[1]], 1), fh_ref[...], fl_ref[...])
    sign = signs()
    prior = jnp.concatenate([jnp.zeros((OWN, 2 * BLOCK), F32), spec[: OWN * (MOST - 1), :]], 0)
    filt[: OWN * MOST, :] = spec + jnp.concatenate(
        [-sign * prior[:, BLOCK:], sign * prior[:, :BLOCK]], 1
    )
    filt[OWN * MOST :, :] = jnp.zeros((OWN * UNROLL, 2 * BLOCK), F32)
    nothing = (jnp.zeros((OWN, LANES), F32),) * 4

    def genome(g, begin):
        count = genome_ref[g]

        def one_block(b, _):
            row = pl.multiple_of(OWN * (begin + b), OWN)
            store4(
                back, row, sweep(filt, 0, carried_ref, begin + UNROLL * g + b, count - b, nothing)
            )
            return 0

        lax.fori_loop(0, count, one_block, 0)
        return begin + count

    lax.fori_loop(0, GENOMES, genome, jnp.int32(0))
    group = 16
    for part in range(NCTX // group):
        rows = dot3(
            back[OWN * group * part : OWN * group * (part + 1), :], ih_ref[...], il_ref[...]
        )
        for i in range(group):
            base = OUT_ROWS * (part * group + i)
            for half in range(2):
                out_ref[base + 8 * half : base + 8 * half + 8, :] = rows[
                    OWN * i : OWN * (i + 1), half * LANES : (half + 1) * LANES
                ]
    for i in range(NCTX):
        base = OUT_ROWS * i + 16
        out_ref[base : base + 4, :] = jnp.zeros((4, LANES), F32)


def unpack_kernel(scale, x_ref, q_ref, k_ref, gq_ref, gk_ref, gf_ref, turned):
    for half in range(2):
        for quarter in range(PLANES):
            for r in range(2):
                rows = x_ref[pl.ds(8 * half + 2 * quarter + r, NCTX, stride=OUT_ROWS), :]
                turned[half, pl.ds(LANES * quarter + r, NCTX, stride=2), :] = rows
        part = slice(half * LANES, (half + 1) * LANES)
        back = turned[half].T
        gq_ref[part, :] = (back * k_ref[part, :].astype(F32)).astype(BF16)
        gk_ref[part, :] = (back * q_ref[part, :].astype(F32)).astype(BF16)
    for half in range(2):
        for r in range(2):
            rows = x_ref[pl.ds(16 + 2 * half + r, NCTX, stride=OUT_ROWS), :]
            turned[half, pl.ds(r, NCTX, stride=2), :] = rows
        gf_ref[half * LANES : (half + 1) * LANES, :] = turned[half, 0:LANES, :].T * scale


VMEM = pl.BlockSpec(memory_space=pltpu.VMEM)
SMEM = pl.BlockSpec(memory_space=pltpu.SMEM)


def params():
    return pltpu.CompilerParams(vmem_limit_bytes=40 * 1024 * 1024)


def cost(flops, moved):
    return pl.CostEstimate(flops=flops, bytes_accessed=moved, transcendentals=0)


def shape(*dims):
    return jax.ShapeDtypeStruct(dims, F32)


def pack(q, k, v, g, f):
    return pl.pallas_call(
        pack_kernel,
        out_shape=shape(NCTX * IN_ROWS, LANES),
        in_specs=[VMEM] * 5,
        out_specs=VMEM,
        scratch_shapes=[pltpu.VMEM((2, 2 * BLOCK, LANES), F32)],
        compiler_params=params(),
        cost_estimate=cost(1 << 20, 3 << 20),
        name="pack",
    )(q, k, v, g, f)


def lag_part(genome_blocks, plane, x, tables):
    return pl.pallas_call(
        lag_kernel,
        out_shape=[
            shape(PLANES, 4 * MOST, LANES),
            shape(OWN * (NCTX + UNROLL * GENOMES), 2 * BLOCK),
        ],
        in_specs=[SMEM, SMEM] + [VMEM] * 5,
        out_specs=[VMEM, VMEM],
        scratch_shapes=[
            pltpu.VMEM((OWN * (NCTX + UNROLL), 2 * BLOCK), F32),
            pltpu.VMEM((OWN * (MOST + 1), 2 * BLOCK), F32),
            pltpu.VMEM((2, OWN * MOST, LANES), F32),
            pltpu.SMEM((NCTX,), jnp.int32),
        ],
        compiler_params=params(),
        cost_estimate=cost(4 << 30, 16 << 20),
        name="lag_part",
    )(genome_blocks, plane, x, *tables)


def back_part(genome_blocks, plane, carried, quarters, tables):
    return pl.pallas_call(
        back_kernel,
        out_shape=shape(NCTX * OUT_ROWS, LANES),
        in_specs=[SMEM, SMEM] + [VMEM] * 9,
        out_specs=VMEM,
        scratch_shapes=[
            pltpu.VMEM((OWN * (MOST + UNROLL), 2 * BLOCK), F32),
            pltpu.VMEM((OWN * NCTX, 2 * BLOCK), F32),
            pltpu.VMEM((2, OWN * MOST, LANES), F32),
        ],
        compiler_params=params(),
        cost_estimate=cost(4 << 30, 16 << 20),
        name="back_part",
    )(genome_blocks, plane, carried, *quarters, *tables)


def unpack(x, q, k, scale):
    half = jax.ShapeDtypeStruct(q.shape, BF16)
    return pl.pallas_call(
        functools.partial(unpack_kernel, scale),
        out_shape=[half, half, shape(BLOCK, LANES)],
        in_specs=[VMEM] * 3,
        out_specs=[VMEM] * 3,
        scratch_shapes=[pltpu.VMEM((2, 2 * BLOCK, LANES), F32)],
        compiler_params=params(),
        cost_estimate=cost(1 << 20, 3 << 20),
        name="unpack",
    )(x, q, k)


def shift(x, k):
    return lax.ppermute(x, "ch", [(i, (i + k) % PLANES) for i in range(PLANES)])


def exchange(x):
    return lax.all_to_all(x, "ctx", split_axis=0, concat_axis=0, tiled=True)


def local(q, k, v, g, c, filters, genome_blocks):
    tables = [jnp.asarray(t) for t in dft_tables()]
    plane = lax.axis_index("ch").astype(jnp.int32)
    plane_arr = plane.reshape(1)
    own_filters = lax.dynamic_slice_in_dim(filters, plane * LANES, LANES, 1)
    grad_value = (g.astype(F32) * c.astype(F32)).astype(BF16)
    sent = pack(q, k, v, g, own_filters).reshape(NCTX, IN_ROWS // 4, 4, LANES)
    got = exchange(sent)
    own_quarter = got[:MOST, 8].reshape(4 * MOST, LANES)
    quarters = [own_quarter] + [shift(own_quarter, i) for i in range(1, PLANES)]
    lag_slots, carried = lag_part(
        genome_blocks, plane_arr, got.reshape(NCTX * IN_ROWS, LANES), tables
    )
    lag_sum = lag_slots[0]
    for i in range(1, PLANES):
        lag_sum = lag_sum + shift(lag_slots[i], i)
    back = back_part(genome_blocks, plane_arr, carried, quarters, tables)
    back = back.reshape(NCTX, OUT_ROWS // 4, 4, LANES)
    back = lax.dynamic_update_slice(back, lag_sum.reshape(MOST, 1, 4, LANES), (0, 4, 0, 0))
    returned = exchange(back).reshape(NCTX * OUT_ROWS, LANES)
    scale = (NCTX * BLOCK) ** (-0.5)
    grad_query, grad_key, grad_filters = unpack(returned, q, k, scale)
    return grad_query, grad_key, grad_value, grad_filters


def solution(mesh):
    split = P("ctx", "ch")
    return jax.shard_map(
        local,
        mesh=mesh,
        in_specs=(split,) * 5 + (P("ctx", None), P()),
        out_specs=(split,) * 4,
        check_vma=False,
    )
```

profile of v0, /device:TPU:1, one launch (start us, length us, event | category | flops | bytes accessed | tf_op | source)
XLA Modules:
  0.0 104.4 jit_solution(17269401002435099884)
XLA Ops:
  0.6 0.0 copy-start
  0.7 1.0 copy-done
  1.7 0.9 copy-done.1
  2.7 0.9 copy-done.3
  3.6 0.9 copy-done.5
  4.6 0.9 copy-done.7
  5.5 0.5 pack.1
  6.0 0.0 copy-start.9
  6.1 43.7 %all_to_all.10 = f32[64,9,4,128]{3,2,1,0:T(4,128)S(1)} all-to-all(f32[64,9,4,128]{3,2,1,0:T(4,128)S(1)} %bitcast.21), channel_id=1, replica_groups=mesh['ctx'=64,'ch'=4] {'ctx'}, dimensions={0} | all-to-all | bytes 2359296 | tf_op jit(solution)/shard_map/all_to_all | solution.py:322
  49.8 6.6 %lag_part.1 = (f32[4,128,128]{2,1,0:T(8,128)S(1)}, f32[768,512]{1,0:T(8,128)S(1)}) custom-call(s32[8]{0:T(128)S(1)} %copy-done.8, s32[1]{0:T(128)} %bitcast.plane_ref, f32[2304,128]{1,0:T(8,128)S(1)} %bitcast.23, bf16[256,512]{1,0:T(8,128)(2,1)S(1)} %copy-done.9, bf16[256,512]{1,0:T(8,128)(2,1)S(1)} %copy-done.10, bf16[512,256]{1,0:T(8,128)(2,1)S(1)} %copy-done.11, ...), custom_call_target="tpu_custom_call" | custom-call | flops 4294967296 | bytes 16777216 | tf_op jit(solution)/shard_map/lag_part/pallas_call | solution.py:266
  56.4 1.3 %collective-permute-start.3 = (f32[128,128]{1,0:T(8,128)S(1)}, f32[128,128]{1,0:T(8,128)S(1)}, u32[]{:S(2)}, u32[]{:S(2)}) collective-permute-start(f32[128,128]{1,0:T(8,128)S(1)} %get-tuple-element.14), channel_id=1, source_target_pairs={{0,1},{1,2},{2,3},{3,0},{4,5},{5,6},{6,7},{7,4},{8,9},{9,10},{10,1... | collective-permute-start | bytes 196616 | tf_op jit(solution)/shard_map/ppermute | solution.py:318
  57.7 2.4 %collective-permute-start.4 = (f32[128,128]{1,0:T(8,128)S(1)}, f32[128,128]{1,0:T(8,128)S(1)}, u32[]{:S(2)}, u32[]{:S(2)}) collective-permute-start(f32[128,128]{1,0:T(8,128)S(1)} %get-tuple-element.16), channel_id=1, source_target_pairs={{0,2},{1,3},{2,0},{3,1},{4,6},{5,7},{6,4},{7,5},{8,10},{9,11},{10,... | collective-permute-start | bytes 196616 | tf_op jit(solution)/shard_map/ppermute | solution.py:318
  60.1 1.2 %collective-permute-start.5 = (f32[128,128]{1,0:T(8,128)S(1)}, f32[128,128]{1,0:T(8,128)S(1)}, u32[]{:S(2)}, u32[]{:S(2)}) collective-permute-start(f32[128,128]{1,0:T(8,128)S(1)} %get-tuple-element.15), channel_id=1, source_target_pairs={{0,3},{1,0},{2,1},{3,2},{4,7},{5,4},{6,5},{7,6},{8,11},{9,8},{10,9... | collective-permute-start | bytes 196616 | tf_op jit(solution)/shard_map/ppermute | solution.py:318
  61.3 0.4 collective-permute-start
  61.7 0.9 collective-permute-start.1
  62.6 1.6 %collective-permute-start.2 = (f32[128,128]{1,0:T(8,128)S(1)}, f32[128,128]{1,0:T(8,128)S(1)}, u32[]{:S(2)}, u32[]{:S(2)}) collective-permute-start(f32[128,128]{1,0:T(8,128)S(1)} %bitcast.26), channel_id=1, source_target_pairs={{0,3},{1,0},{2,1},{3,2},{4,7},{5,4},{6,5},{7,6},{8,11},{9,8},{10,9... | collective-permute-start | bytes 196616 | tf_op jit(solution)/shard_map/ppermute | solution.py:318
  64.2 2.4 %collective-permute-done.f1_ref = f32[128,128]{1,0:T(8,128)S(1)} collective-permute-done((f32[128,128]{1,0:T(8,128)S(1)}, f32[128,128]{1,0:T(8,128)S(1)}, u32[]{:S(2)}, u32[]{:S(2)}) %collective-permute-start) | collective-permute-done | bytes 65568 | tf_op jit(solution)/shard_map/ppermute | solution.py:318
  66.6 0.6 collective-permute-done.2.f3_ref
  67.2 6.4 %back_part.1 = f32[1280,128]{1,0:T(8,128)} custom-call(s32[8]{0:T(128)S(1)} %copy-done.8, s32[1]{0:T(128)} %bitcast.plane_ref, f32[768,512]{1,0:T(8,128)S(1)} %get-tuple-element.9.carried_ref, f32[128,128]{1,0:T(8,128)S(1)} %bitcast.27, f32[128,128]{1,0:T(8,128)S(1)} %collective-permute-done.f1_ref, f32[128,128]{1,0:T(8,128)S(1)} %collective-permute-done.1.f2_ref, ...), custom_call_target="tpu_custom_call" | custom-call | flops 4294967296 | bytes 16777216 | tf_op jit(solution)/shard_map/back_part/pallas_call | solution.py:287
  73.6 0.7 constant_dynamic-update-slice_fusion
  74.3 8.7 %all-to-all-start.1 = ((f32[64,5,4,128]{3,2,1,0:T(4,128)}), f32[64,5,4,128]{3,2,1,0:T(4,128)S(1)}, u32[]{:S(2)}, u32[]{:S(2)}) async-start(f32[64,5,4,128]{3,2,1,0:T(4,128)} %constant_dynamic-update-slice_fusion), calls=%async_computation.1 | async-start | bytes 1310720 | tf_op jit(solution)/shard_map/all_to_all | solution.py:322
  83.0 0.8 multiply_convert_fusion
  83.7 19.6 %all-to-all-done.1 = f32[64,5,4,128]{3,2,1,0:T(4,128)S(1)} async-done(((f32[64,5,4,128]{3,2,1,0:T(4,128)}), f32[64,5,4,128]{3,2,1,0:T(4,128)S(1)}, u32[]{:S(2)}, u32[]{:S(2)}) %all-to-all-start.1) | async-done | bytes 655392 | tf_op jit(solution)/shard_map/all_to_all | solution.py:322
  103.3 1.1 %unpack.1 = (bf16[256,512]{1,0:T(8,128)(2,1)}, bf16[256,512]{1,0:T(8,128)(2,1)}, f32[256,128]{1,0:T(8,128)}) custom-call(f32[1280,128]{1,0:T(8,128)S(1)} %bitcast.22, bf16[256,512]{1,0:T(8,128)(2,1)S(1)} %copy-done.4, bf16[256,512]{1,0:T(8,128)(2,1)S(1)} %copy-done.6), custom_call_target="tpu_custom_call" | custom-call | flops 1048576 | bytes 3145728 | tf_op jit(solution)/shard_map/unpack/pallas_call | solution.py:305
  (29 shorter events, 0.1 us)
Async XLA Ops:
  0.6 1.0 %copy-start = (f32[256,512]{1,0:T(8,128)S(1)}, f32[256,512]{1,0:T(8,128)}, u32[]{:S(2)}) copy-start(f32[256,512]{1,0:T(8,128)} %param.16) | copy-start | bytes 1572868
  1.7 1.0 copy-start.1
  2.7 0.9 copy-start.3
  3.6 0.9 copy-start.5
  4.6 0.9 copy-start.7
  6.0 43.7 %copy-start.8 = (s32[8]{0:T(128)S(1)}, s32[8]{0:T(128)}, u32[]{:S(2)}) copy-start(s32[8]{0:T(128)} %genome_ref.3) | copy-start | bytes 100
  6.0 43.7 %copy-start.9 = (bf16[256,512]{1,0:T(8,128)(2,1)S(1)}, bf16[256,512]{1,0:T(8,128)(2,1)}, u32[]{:S(2)}) copy-start(bf16[256,512]{1,0:T(8,128)(2,1)} %constant.20.clone.fh_ref) | copy-start | bytes 786436
  6.0 43.7 %copy-start.10 = (bf16[256,512]{1,0:T(8,128)(2,1)S(1)}, bf16[256,512]{1,0:T(8,128)(2,1)}, u32[]{:S(2)}) copy-start(bf16[256,512]{1,0:T(8,128)(2,1)} %constant.21.clone.fl_ref) | copy-start | bytes 786436
  6.0 43.7 %copy-start.11 = (bf16[512,256]{1,0:T(8,128)(2,1)S(1)}, bf16[512,256]{1,0:T(8,128)(2,1)}, u32[]{:S(2)}) copy-start(bf16[512,256]{1,0:T(8,128)(2,1)} %constant.22.clone.ih_ref) | copy-start | bytes 786436
  6.0 43.7 %copy-start.12 = (bf16[512,256]{1,0:T(8,128)(2,1)S(1)}, bf16[512,256]{1,0:T(8,128)(2,1)}, u32[]{:S(2)}) copy-start(bf16[512,256]{1,0:T(8,128)(2,1)} %constant.23.clone.il_ref) | copy-start | bytes 786436
  56.4 6.2 %collective-permute-start.3 = (f32[128,128]{1,0:T(8,128)S(1)}, f32[128,128]{1,0:T(8,128)S(1)}, u32[]{:S(2)}, u32[]{:S(2)}) collective-permute-start(f32[128,128]{1,0:T(8,128)S(1)} %get-tuple-element.14), channel_id=1, source_target_pairs={{0,1},{1,2},{2,3},{3,0},{4,5},{5,6},{6,7},{7,4},{8,9},{9,10},{10,1... | collective-permute-start | bytes 196616 | tf_op jit(solution)/shard_map/ppermute | solution.py:318
  57.7 6.5 %collective-permute-start.4 = (f32[128,128]{1,0:T(8,128)S(1)}, f32[128,128]{1,0:T(8,128)S(1)}, u32[]{:S(2)}, u32[]{:S(2)}) collective-permute-start(f32[128,128]{1,0:T(8,128)S(1)} %get-tuple-element.16), channel_id=1, source_target_pairs={{0,2},{1,3},{2,0},{3,1},{4,6},{5,7},{6,4},{7,5},{8,10},{9,11},{10,... | collective-permute-start | bytes 196616 | tf_op jit(solution)/shard_map/ppermute | solution.py:318
  60.1 4.1 %collective-permute-start.5 = (f32[128,128]{1,0:T(8,128)S(1)}, f32[128,128]{1,0:T(8,128)S(1)}, u32[]{:S(2)}, u32[]{:S(2)}) collective-permute-start(f32[128,128]{1,0:T(8,128)S(1)} %get-tuple-element.15), channel_id=1, source_target_pairs={{0,3},{1,0},{2,1},{3,2},{4,7},{5,4},{6,5},{7,6},{8,11},{9,8},{10,9... | collective-permute-start | bytes 196616 | tf_op jit(solution)/shard_map/ppermute | solution.py:318
  61.3 5.3 %collective-permute-start = (f32[128,128]{1,0:T(8,128)S(1)}, f32[128,128]{1,0:T(8,128)S(1)}, u32[]{:S(2)}, u32[]{:S(2)}) collective-permute-start(f32[128,128]{1,0:T(8,128)S(1)} %bitcast.24), channel_id=1, source_target_pairs={{0,1},{1,2},{2,3},{3,0},{4,5},{5,6},{6,7},{7,4},{8,9},{9,10},{10,1... | collective-permute-start | bytes 196616 | tf_op jit(solution)/shard_map/ppermute | solution.py:318
  61.7 4.9 %collective-permute-start.1 = (f32[128,128]{1,0:T(8,128)S(1)}, f32[128,128]{1,0:T(8,128)S(1)}, u32[]{:S(2)}, u32[]{:S(2)}) collective-permute-start(f32[128,128]{1,0:T(8,128)S(1)} %bitcast.25), channel_id=1, source_target_pairs={{0,2},{1,3},{2,0},{3,1},{4,6},{5,7},{6,4},{7,5},{8,10},{9,11},{10,... | collective-permute-start | bytes 196616 | tf_op jit(solution)/shard_map/ppermute | solution.py:318
  62.6 4.7 %collective-permute-start.2 = (f32[128,128]{1,0:T(8,128)S(1)}, f32[128,128]{1,0:T(8,128)S(1)}, u32[]{:S(2)}, u32[]{:S(2)}) collective-permute-start(f32[128,128]{1,0:T(8,128)S(1)} %bitcast.26), channel_id=1, source_target_pairs={{0,3},{1,0},{2,1},{3,2},{4,7},{5,4},{6,5},{7,6},{8,11},{9,8},{10,9... | collective-permute-start | bytes 196616 | tf_op jit(solution)/shard_map/ppermute | solution.py:318
  73.6 9.3 %copy-start.2 = (bf16[256,512]{1,0:T(8,128)(2,1)S(1)}, bf16[256,512]{1,0:T(8,128)(2,1)}, u32[]{:S(2)}) copy-start(bf16[256,512]{1,0:T(8,128)(2,1)} %g_ref.1) | copy-start | bytes 786436
  73.6 9.3 %copy-start.13 = (bf16[256,512]{1,0:T(8,128)(2,1)S(1)}, bf16[256,512]{1,0:T(8,128)(2,1)}, u32[]{:S(2)}) copy-start(bf16[256,512]{1,0:T(8,128)(2,1)} %param.15) | copy-start | bytes 786436
  73.6 29.7 %copy-start.4 = (bf16[256,512]{1,0:T(8,128)(2,1)S(1)}, bf16[256,512]{1,0:T(8,128)(2,1)}, u32[]{:S(2)}) copy-start(bf16[256,512]{1,0:T(8,128)(2,1)} %q_ref.3) | copy-start | bytes 786436
  73.6 29.7 %copy-start.6 = (bf16[256,512]{1,0:T(8,128)(2,1)S(1)}, bf16[256,512]{1,0:T(8,128)(2,1)}, u32[]{:S(2)}) copy-start(bf16[256,512]{1,0:T(8,128)(2,1)} %k_ref.3) | copy-start | bytes 786436
  74.3 29.0 %all-to-all-start.1 = ((f32[64,5,4,128]{3,2,1,0:T(4,128)}), f32[64,5,4,128]{3,2,1,0:T(4,128)S(1)}, u32[]{:S(2)}, u32[]{:S(2)}) async-start(f32[64,5,4,128]{3,2,1,0:T(4,128)} %constant_dynamic-update-slice_fusion), calls=%async_computation.1 | async-start | bytes 1310720 | tf_op jit(solution)/shard_map/all_to_all | solution.py:322
where the time goes:
time: 105 us; the launch traced here: 104 us
  blocking collectives  43.7 us (42%)
  waiting for transfers between devices  22.6 us (22%)
  starting transfers between devices  16.4 us (16%)
  Pallas kernels  14.5 us (14%)
  local copies, waits for them, and re-layouts  5.57 us (5%)
    all_to_all x1, blocking collectives, exchange(): return lax.all_to_all(x, 'ctx', split_axis=0, concat_axis=0, tiled=True)  43.7 us
    all_to_all x1, waiting for transfers between devices, exchange(): return lax.all_to_all(x, 'ctx', split_axis=0, concat_axis=0, tiled=True)  19.6 us
    all_to_all x1, starting transfers between devices, exchange(): return lax.all_to_all(x, 'ctx', split_axis=0, concat_axis=0, tiled=True)  8.66 us
    ppermute x6, starting transfers between devices, shift(): return lax.ppermute(x, 'ch', [(i, (i + k) % PLANES) for i in range(PLANES)])  7.78 us
    pallas_call x1, Pallas kernels, lag_part(): pl.pallas_call(lag_kernel, out_shape=[shape(PLANES, 4 * MOST, LANES), sha...  6.6 us
    pallas_call x1, Pallas kernels, back_part(): pl.pallas_call(back_kernel, out_shape=shape(NCTX * OUT_ROWS, LANES), in_s...  6.37 us
    unnamed x28, local copies, waits for them, and re-layouts  4.88 us
    ppermute x6, waiting for transfers between devices, shift(): return lax.ppermute(x, 'ch', [(i, (i + k) % PLANES) for i in range(PLANES)])  3.02 us
  transfers between devices with their start and end apart: 7, of which 3 were waited for; matrix products, arithmetic and copies ran while one was open for 1% of the time, Pallas kernels for 0%

commit v1 on v0

v1 whole, which is shorter than its diff:
```python
import functools

import jax
import jax.numpy as jnp
import ml_dtypes
import numpy as np
from jax import lax
from jax.experimental import pallas as pl
from jax.experimental.pallas import tpu as pltpu
from jax.sharding import PartitionSpec as P

BLOCK = 256
LANES = 128
OWN = 8
PLANES = 4
NCTX = 64
MOST = 32
GENOMES = 8
UNROLL = 4
GAP = UNROLL + 1
IN_ROWS = 36
OUT_ROWS = 20
F32 = jnp.float32
BF16 = jnp.bfloat16


def split_table(table):
    high = table.astype(ml_dtypes.bfloat16)
    low = (table - high.astype(np.float64)).astype(ml_dtypes.bfloat16)
    return np.concatenate([high, low, high], axis=0)


def dft_tables():
    freq = np.arange(BLOCK)
    sample = np.arange(BLOCK)
    phase = (sample[:, None] * (2 * freq[None, :] + 1)) % (4 * BLOCK)
    angle = phase * (np.pi / (2 * BLOCK))
    forward = np.concatenate([np.cos(angle), -np.sin(angle)], axis=1)
    return split_table(forward), split_table(forward.T / BLOCK)


def dot3(x, table):
    high = x.astype(BF16)
    low = (x - high.astype(F32)).astype(BF16)
    return jnp.dot(
        jnp.concatenate([low, high, high], 1), table[...], preferred_element_type=F32
    )


def pack_kernel(
    plane_ref, q_hbm, k_hbm, v_hbm, g_hbm, f_hbm, out_ref, q_ref, k_ref, v_ref, g_ref, f_ref,
    turned, sems,
):
    column = pl.multiple_of(plane_ref[0] * LANES, LANES)
    pairs = (
        (g_hbm, g_ref), (v_hbm, v_ref), (q_hbm, q_ref), (k_hbm, k_ref),
        (f_hbm.at[:, pl.ds(column, LANES)], f_ref),
    )
    copies = [pltpu.make_async_copy(a, b, sems.at[i]) for i, (a, b) in enumerate(pairs)]
    for copy in copies:
        copy.start()
    for which, (a_ref, b_ref, first_copy) in enumerate(((g_ref, v_ref, 0), (q_ref, k_ref, 2))):
        copies[first_copy].wait()
        copies[first_copy + 1].wait()
        product = a_ref[...].astype(F32) * b_ref[...].astype(F32)
        for half in range(2):
            turned[half] = product[half * LANES : (half + 1) * LANES, :].T
        for half in range(2):
            for quarter in range(PLANES):
                for r in range(2):
                    rows = turned[half, pl.ds(LANES * quarter + r, NCTX, stride=2), :]
                    first = 16 * (1 - which) + 8 * half + 2 * quarter + r
                    out_ref[pl.ds(first, NCTX, stride=IN_ROWS), :] = rows
    copies[4].wait()
    for half in range(2):
        turned[half, 0:LANES, :] = f_ref[half * LANES : (half + 1) * LANES, :].T
        for r in range(2):
            rows = turned[half, pl.ds(r, NCTX, stride=2), :]
            out_ref[pl.ds(32 + 2 * half + r, NCTX, stride=IN_ROWS), :] = rows


def signs():
    lane = lax.broadcasted_iota(jnp.int32, (1, BLOCK), 1)
    return (1 - 2 * (lane % 2)).astype(F32)


def load4(ref, row):
    return [ref[pl.ds(row, OWN), pl.ds(LANES * i, LANES)] for i in range(4)]


def store4(ref, row, values):
    for i in range(4):
        ref[pl.ds(row, OWN), pl.ds(LANES * i, LANES)] = values[i]


def add_conj(total, first, second):
    out = list(total)
    for i in range(2):
        a_re, a_im, b_re, b_im = first[i], first[i + 2], second[i], second[i + 2]
        out[i] = out[i] + (a_re * b_re + a_im * b_im)
        out[i + 2] = out[i + 2] + (a_re * b_im - a_im * b_re)
    return tuple(out)


def lag_kernel(
    genome_ref, plane_ref, x_ref, fwd_ref, inv_ref, lag_ref, carried_ref, gated, lags, flat, place,
):
    def mark(g, begin):
        count = genome_ref[g]

        def one(b, _):
            place[begin + b] = begin + b + GAP * g
            return 0

        lax.fori_loop(0, count, one, 0)
        row = pl.multiple_of(OWN * (begin + count + GAP * g), OWN)
        carried_ref[pl.ds(row, OWN * GAP), :] = jnp.zeros((OWN * GAP, 2 * BLOCK), F32)
        return begin + count

    lax.fori_loop(0, GENOMES, mark, jnp.int32(0))
    lags[...] = jnp.zeros_like(lags)
    gated[OWN * NCTX :, :] = jnp.zeros((OWN * UNROLL, 2 * BLOCK), F32)
    group = 32
    for part in range(NCTX // group):
        for which in range(2):
            rows = []
            for s in range(part * group, (part + 1) * group):
                base = IN_ROWS * s + 16 * which
                rows.append(
                    jnp.concatenate([x_ref[base : base + 8, :], x_ref[base + 8 : base + 16, :]], 1)
                )
            spec = dot3(jnp.concatenate(rows, 0), fwd_ref)
            if which == 0:
                gated[OWN * group * part : OWN * group * (part + 1), :] = spec
            else:
                for i in range(group):
                    row = pl.multiple_of(OWN * place[part * group + i], OWN)
                    carried_ref[pl.ds(row, OWN), :] = spec[OWN * i : OWN * (i + 1), :]

    def genome(g, begin):
        count = genome_ref[g]
        first = begin + GAP * g

        def two_lags(half, _):
            d = 2 * half

            def step(c, totals):
                low, high = totals
                s = UNROLL * c
                after = load4(carried_ref, pl.multiple_of(OWN * (first + d + s), OWN))
                for u in range(UNROLL):
                    a = load4(gated, pl.multiple_of(OWN * (begin + s + u), OWN))
                    low = add_conj(low, a, after)
                    after = load4(
                        carried_ref, pl.multiple_of(OWN * (first + d + s + u + 1), OWN)
                    )
                    high = add_conj(high, a, after)
                return low, high

            row = pl.multiple_of(OWN * d, OWN)
            start = (tuple(load4(lags, row)), tuple(load4(lags, row + OWN)))
            chunks = (count - d + UNROLL - 1) // UNROLL
            low, high = lax.fori_loop(0, chunks, step, start)
            store4(lags, row, low)
            store4(lags, row + OWN, high)
            return 0

        lax.fori_loop(0, (count + 1) // 2, two_lags, 0)
        return begin + count

    lax.fori_loop(0, GENOMES, genome, jnp.int32(0))
    sign = signs()
    here, after = lags[: OWN * MOST, :], lags[OWN : OWN * (MOST + 1), :]
    spec = jnp.concatenate(
        [here[:, :BLOCK] + sign * after[:, BLOCK:], here[:, BLOCK:] - sign * after[:, :BLOCK]], 1
    )
    rows = dot3(spec, inv_ref)
    for half in range(2):
        flat[half] = rows[:, half * LANES : (half + 1) * LANES]
    for quarter in range(PLANES):
        slot = lax.rem(quarter + PLANES - plane_ref[0], PLANES)
        for half in range(2):
            for r in range(2):
                rows = flat[half, pl.ds(2 * quarter + r, MOST, stride=OWN), :]
                lag_ref[slot, pl.ds(2 * half + r, MOST, stride=4), :] = rows


def back_kernel(
    genome_ref, plane_ref, carried_ref, f0_ref, f1_ref, f2_ref, f3_ref, fwd_ref, back, filt, flat,
):
    for k, f_ref in enumerate((f0_ref, f1_ref, f2_ref, f3_ref)):
        quarter = lax.rem(plane_ref[0] + PLANES - k, PLANES)
        for half in range(2):
            for r in range(2):
                rows = f_ref[pl.ds(2 * half + r, MOST, stride=4), :]
                flat[half, pl.ds(2 * quarter + r, MOST, stride=OWN), :] = rows
    spec = dot3(jnp.concatenate([flat[0], flat[1]], 1), fwd_ref)
    sign = signs()
    prior = jnp.concatenate([jnp.zeros((OWN, 2 * BLOCK), F32), spec[: OWN * (MOST - 1), :]], 0)
    filt[:OWN, :] = jnp.zeros((OWN, 2 * BLOCK), F32)
    filt[OWN : OWN * (MOST + 1), :] = spec + jnp.concatenate(
        [-sign * prior[:, BLOCK:], sign * prior[:, :BLOCK]], 1
    )
    filt[OWN * (MOST + 1) :, :] = jnp.zeros((OWN * UNROLL, 2 * BLOCK), F32)
    nothing = (jnp.zeros((OWN, LANES), F32),) * 4

    def genome(g, begin):
        count = genome_ref[g]
        first = begin + GAP * g

        def two_blocks(half, _):
            b = 2 * half

            def step(c, totals):
                low, high = totals
                t = UNROLL * c
                before = load4(filt, pl.multiple_of(OWN * t, OWN))
                for u in range(UNROLL):
                    later = load4(carried_ref, pl.multiple_of(OWN * (first + b + t + u), OWN))
                    high = add_conj(high, before, later)
                    before = load4(filt, pl.multiple_of(OWN * (t + u + 1), OWN))
                    low = add_conj(low, before, later)
                return low, high

            chunks = (count - b + UNROLL - 1) // UNROLL
            low, high = lax.fori_loop(0, chunks, step, (nothing, nothing))
            row = pl.multiple_of(OWN * (begin + b), OWN)
            store4(back, row, low)
            store4(back, row + OWN, high)
            return 0

        lax.fori_loop(0, (count + 1) // 2, two_blocks, 0)
        return begin + count

    lax.fori_loop(0, GENOMES, genome, jnp.int32(0))


def finish_kernel(back, l0_ref, l1_ref, l2_ref, l3_ref, inv_ref, out_ref):
    group = 32
    for part in range(NCTX // group):
        rows = dot3(back[OWN * group * part : OWN * group * (part + 1), :], inv_ref)
        for i in range(group):
            base = OUT_ROWS * (part * group + i)
            for half in range(2):
                out_ref[base + 8 * half : base + 8 * half + 8, :] = rows[
                    OWN * i : OWN * (i + 1), half * LANES : (half + 1) * LANES
                ]
    for i in range(MOST):
        part = slice(4 * i, 4 * i + 4)
        total = (l0_ref[part, :] + l1_ref[part, :]) + (l2_ref[part, :] + l3_ref[part, :])
        out_ref[OUT_ROWS * i + 16 : OUT_ROWS * i + 20, :] = total
    for i in range(MOST, NCTX):
        out_ref[OUT_ROWS * i + 16 : OUT_ROWS * i + 20, :] = jnp.zeros((4, LANES), F32)


def unpack_kernel(scale, x_ref, q_ref, k_ref, gq_ref, gk_ref, gf_ref, turned):
    for half in range(2):
        for quarter in range(PLANES):
            for r in range(2):
                rows = x_ref[pl.ds(8 * half + 2 * quarter + r, NCTX, stride=OUT_ROWS), :]
                turned[half, pl.ds(LANES * quarter + r, NCTX, stride=2), :] = rows
        part = slice(half * LANES, (half + 1) * LANES)
        back = turned[half].T
        gq_ref[part, :] = (back * k_ref[part, :].astype(F32)).astype(BF16)
        gk_ref[part, :] = (back * q_ref[part, :].astype(F32)).astype(BF16)
    for half in range(2):
        for r in range(2):
            rows = x_ref[pl.ds(16 + 2 * half + r, NCTX, stride=OUT_ROWS), :]
            turned[half, pl.ds(r, NCTX, stride=2), :] = rows
        gf_ref[half * LANES : (half + 1) * LANES, :] = turned[half, 0:LANES, :].T * scale


VMEM = pl.BlockSpec(memory_space=pltpu.VMEM)
SMEM = pl.BlockSpec(memory_space=pltpu.SMEM)
HBM = pl.BlockSpec(memory_space=pltpu.HBM)


def params(mib=40):
    return pltpu.CompilerParams(vmem_limit_bytes=mib * 1024 * 1024)


def cost(flops, moved):
    return pl.CostEstimate(flops=flops, bytes_accessed=moved, transcendentals=0)


def shape(*dims):
    return jax.ShapeDtypeStruct(dims, F32)


def pack(plane, q, k, v, g, f):
    half = pltpu.VMEM(q.shape, BF16)
    return pl.pallas_call(
        pack_kernel,
        out_shape=shape(NCTX * IN_ROWS, LANES),
        in_specs=[SMEM] + [HBM] * 5,
        out_specs=VMEM,
        scratch_shapes=[half] * 4
        + [
            pltpu.VMEM((BLOCK, LANES), F32),
            pltpu.VMEM((2, 2 * BLOCK, LANES), F32),
            pltpu.SemaphoreType.DMA((5,)),
        ],
        compiler_params=params(60),
        cost_estimate=cost(1 << 20, 3 << 20),
        name="pack",
    )(plane, q, k, v, g, f)


def lag_part(genome_blocks, plane, x, tables):
    return pl.pallas_call(
        lag_kernel,
        out_shape=[
            shape(PLANES, 4 * MOST, LANES),
            shape(OWN * (NCTX + GAP * GENOMES), 2 * BLOCK),
        ],
        in_specs=[SMEM, SMEM] + [VMEM] * 3,
        out_specs=[VMEM, VMEM],
        scratch_shapes=[
            pltpu.VMEM((OWN * (NCTX + UNROLL), 2 * BLOCK), F32),
            pltpu.VMEM((OWN * (MOST + 1), 2 * BLOCK), F32),
            pltpu.VMEM((2, OWN * MOST, LANES), F32),
            pltpu.SMEM((NCTX,), jnp.int32),
        ],
        compiler_params=params(),
        cost_estimate=cost(1 << 36, 16 << 20),
        name="lag_part",
    )(genome_blocks, plane, x, *tables)


def back_part(genome_blocks, plane, carried, quarters, table):
    return pl.pallas_call(
        back_kernel,
        out_shape=shape(OWN * (NCTX + 1), 2 * BLOCK),
        in_specs=[SMEM, SMEM] + [VMEM] * 6,
        out_specs=VMEM,
        scratch_shapes=[
            pltpu.VMEM((OWN * (MOST + 1 + UNROLL), 2 * BLOCK), F32),
            pltpu.VMEM((2, OWN * MOST, LANES), F32),
        ],
        compiler_params=params(),
        cost_estimate=cost(1 << 36, 16 << 20),
        name="back_part",
    )(genome_blocks, plane, carried, *quarters, table)


def finish(back, lags, table):
    return pl.pallas_call(
        finish_kernel,
        out_shape=shape(NCTX * OUT_ROWS, LANES),
        in_specs=[VMEM] * 6,
        out_specs=VMEM,
        compiler_params=params(),
        cost_estimate=cost(1 << 28, 4 << 20),
        name="finish",
    )(back, *lags, table)


def unpack(x, q, k, scale):
    half = jax.ShapeDtypeStruct(q.shape, BF16)
    return pl.pallas_call(
        functools.partial(unpack_kernel, scale),
        out_shape=[half, half, shape(BLOCK, LANES)],
        in_specs=[VMEM] * 3,
        out_specs=[VMEM] * 3,
        scratch_shapes=[pltpu.VMEM((2, 2 * BLOCK, LANES), F32)],
        compiler_params=params(),
        cost_estimate=cost(1 << 20, 3 << 20),
        name="unpack",
    )(x, q, k)


def shift(x, k):
    return lax.ppermute(x, "ch", [(i, (i + k) % PLANES) for i in range(PLANES)])


def exchange(x):
    return lax.all_to_all(x, "ctx", split_axis=0, concat_axis=0, tiled=True)


def local(q, k, v, g, c, filters, genome_blocks):
    forward, inverse = [jnp.asarray(t) for t in dft_tables()]
    plane = lax.axis_index("ch").astype(jnp.int32).reshape(1)
    grad_value = (g.astype(F32) * c.astype(F32)).astype(BF16)
    sent = pack(plane, q, k, v, g, filters).reshape(NCTX, IN_ROWS // 4, 4, LANES)
    got = exchange(sent)
    own_quarter = got[:MOST, 8].reshape(4 * MOST, LANES)
    quarters = [own_quarter] + [shift(own_quarter, i) for i in range(1, PLANES)]
    slots, carried = lag_part(
        genome_blocks, plane, got.reshape(NCTX * IN_ROWS, LANES), (forward, inverse)
    )
    lags = [slots[0]] + [shift(slots[i], i) for i in range(1, PLANES)]
    back = back_part(genome_blocks, plane, carried, quarters, forward)
    out = finish(back, lags, inverse).reshape(NCTX, OUT_ROWS // 4, 4, LANES)
    returned = exchange(out).reshape(NCTX * OUT_ROWS, LANES)
    scale = (NCTX * BLOCK) ** (-0.5)
    grad_query, grad_key, grad_filters = unpack(returned, q, k, scale)
    return grad_query, grad_key, grad_value, grad_filters


def solution(mesh):
    split = P("ctx", "ch")
    return jax.shard_map(
        local,
        mesh=mesh,
        in_specs=(split,) * 5 + (P("ctx", None), P()),
        out_specs=(split,) * 4,
        check_vma=False,
    )
```

time: 105 us -> 96.3 us (0.917)
  local copies, waits for them, and re-layouts: 5.57 us -> 0.07 us
  waiting for transfers between devices: 22.6 us -> 19.6 us
    unnamed x28 -> x14, local copies, waits for them, and re-layouts: 4.88 us -> 0.03 us
    ppermute x6, waiting for transfers between devices: 3.02 us -> 0.02 us  [shift(): return lax.ppermute(x, 'ch', [(i, (i + k) % PLANES) for i in range(PLANES)])]
    pallas_call x1, Pallas kernels: 0.49 us -> 2.78 us  [pack(): pl.pallas_call(pack_kernel, out_shape=shape(NCTX * IN_ROWS, LANES), in_sp...]
    pallas_call x1 -> x2, Pallas kernels: 6.37 us -> 5.36 us  [the longest x1 3.91 us: back_part(): pl.pallas_call(back_kernel, out_shape=shape(OWN * (NCTX + 1), 2 * BLOCK),...]
  transfers between devices with their start and end apart: 7 -> 7, of which waited for: 3 -> 1; matrix products, arithmetic and copies ran while one was open for 1% -> 1% of each run, Pallas kernels for 0% -> 10%
where the time goes in v1:
time: 96.3 us; the launch traced here: 96 us
  blocking collectives  43.9 us (46%)
  waiting for transfers between devices  19.6 us (20%)
  starting transfers between devices  15.9 us (17%)
  Pallas kernels  15 us (16%)
    all_to_all x1, blocking collectives, exchange(): return lax.all_to_all(x, 'ctx', split_axis=0, concat_axis=0, tiled=True)  43.9 us
    all_to_all x1, waiting for transfers between devices, exchange(): return lax.all_to_all(x, 'ctx', split_axis=0, concat_axis=0, tiled=True)  19.6 us
    all_to_all x1, starting transfers between devices, exchange(): return lax.all_to_all(x, 'ctx', split_axis=0, concat_axis=0, tiled=True)  8.17 us
    ppermute x6, starting transfers between devices, shift(): return lax.ppermute(x, 'ch', [(i, (i + k) % PLANES) for i in range(PLANES)])  7.77 us
    pallas_call x1, Pallas kernels, lag_part(): pl.pallas_call(lag_kernel, out_shape=[shape(PLANES, 4 * MOST, LANES), sha...  5.78 us
    pallas_call x1, Pallas kernels, back_part(): pl.pallas_call(back_kernel, out_shape=shape(OWN * (NCTX + 1), 2 * BLOCK),...  3.91 us
    pallas_call x1, Pallas kernels, pack(): pl.pallas_call(pack_kernel, out_shape=shape(NCTX * IN_ROWS, LANES), in_sp...  2.78 us
  transfers between devices with their start and end apart: 7, of which 1 were waited for; matrix products, arithmetic and copies ran while one was open for 1% of the time, Pallas kernels for 10%

profile of v1, /device:TPU:1, one launch (start us, length us, event | category | flops | bytes accessed | tf_op | source)
XLA Modules:
  0.0 96.0 jit_solution(11207914387403628207)
XLA Ops:
  0.6 2.8 %pack.1 = f32[2304,128]{1,0:T(8,128)} custom-call(s32[1]{0:T(128)} %bitcast.plane_ref, bf16[256,512]{1,0:T(8,128)(2,1)} %q_ref.1, bf16[256,512]{1,0:T(8,128)(2,1)} %k_ref.1, bf16[256,512]{1,0:T(8,128)(2,1)} %v_hbm.1, bf16[256,512]{1,0:T(8,128)(2,1)} %g_hbm.1, f32[256,512]{1,0:T(8,128)} %f_hbm.1), custom_call_target="tpu_custom_call" | custom-call | flops 1048576 | bytes 3145728 | tf_op jit(solution)/shard_map/pack/pallas_call | solution.py:292
  3.4 0.0 copy-start.2
  3.4 0.0 copy-start.3
  3.4 0.0 copy-start.4
  3.5 43.9 %all_to_all.10 = f32[64,9,4,128]{3,2,1,0:T(4,128)S(1)} all-to-all(f32[64,9,4,128]{3,2,1,0:T(4,128)} %bitcast.20), channel_id=1, replica_groups=mesh['ctx'=64,'ch'=4] {'ctx'}, dimensions={0} | all-to-all | bytes 2359296 | tf_op jit(solution)/shard_map/all_to_all | solution.py:377
  47.4 1.3 %collective-permute-start = (f32[128,128]{1,0:T(8,128)S(1)}, f32[128,128]{1,0:T(8,128)S(1)}, u32[]{:S(2)}, u32[]{:S(2)}) collective-permute-start(f32[128,128]{1,0:T(8,128)S(1)} %bitcast.16), channel_id=1, source_target_pairs={{0,1},{1,2},{2,3},{3,0},{4,5},{5,6},{6,7},{7,4},{8,9},{9,10},{10,1... | collective-permute-start | bytes 196616 | tf_op jit(solution)/shard_map/ppermute | solution.py:373
  48.7 2.5 %collective-permute-start.1 = (f32[128,128]{1,0:T(8,128)S(1)}, f32[128,128]{1,0:T(8,128)S(1)}, u32[]{:S(2)}, u32[]{:S(2)}) collective-permute-start(f32[128,128]{1,0:T(8,128)S(1)} %bitcast.17), channel_id=1, source_target_pairs={{0,2},{1,3},{2,0},{3,1},{4,6},{5,7},{6,4},{7,5},{8,10},{9,11},{10,... | collective-permute-start | bytes 196616 | tf_op jit(solution)/shard_map/ppermute | solution.py:373
  51.1 1.2 %collective-permute-start.2 = (f32[128,128]{1,0:T(8,128)S(1)}, f32[128,128]{1,0:T(8,128)S(1)}, u32[]{:S(2)}, u32[]{:S(2)}) collective-permute-start(f32[128,128]{1,0:T(8,128)S(1)} %bitcast.18), channel_id=1, source_target_pairs={{0,3},{1,0},{2,1},{3,2},{4,7},{5,4},{6,5},{7,6},{8,11},{9,8},{10,9... | collective-permute-start | bytes 196616 | tf_op jit(solution)/shard_map/ppermute | solution.py:373
  52.3 5.8 %lag_part.1 = (f32[4,128,128]{2,1,0:T(8,128)S(1)}, f32[832,512]{1,0:T(8,128)S(1)}) custom-call(s32[8]{0:T(128)S(1)} %copy-done.3, s32[1]{0:T(128)} %bitcast.plane_ref, f32[2304,128]{1,0:T(8,128)S(1)} %bitcast.15, bf16[768,512]{1,0:T(8,128)(2,1)S(1)} %copy-done.4, bf16[1536,256]{1,0:T(8,128)(2,1)S(1)} %copy-done.2), custom_call_target="tpu_custom_call" | custom-call | flops 68719476736 | bytes 16777216 | tf_op jit(solution)/shard_map/lag_part/pallas_call | solution.py:310
  58.1 0.4 collective-permute-start.3
  58.5 0.9 collective-permute-start.4
  59.4 0.0 collective-permute-done.f1_ref
  59.4 1.6 %collective-permute-start.5 = (f32[128,128]{1,0:T(8,128)S(1)}, f32[128,128]{1,0:T(8,128)S(1)}, u32[]{:S(2)}, u32[]{:S(2)}) collective-permute-start(f32[128,128]{1,0:T(8,128)S(1)} %get-tuple-element.14), channel_id=1, source_target_pairs={{0,3},{1,0},{2,1},{3,2},{4,7},{5,4},{6,5},{7,6},{8,11},{9,8},{10,9... | collective-permute-start | bytes 196616 | tf_op jit(solution)/shard_map/ppermute | solution.py:373
  61.0 0.0 collective-permute-done.1.f2_ref
  61.0 0.0 collective-permute-done.2.f3_ref
  61.0 3.9 %back_part.1.back = f32[520,512]{1,0:T(8,128)S(1)} custom-call(s32[8]{0:T(128)S(1)} %copy-done.3, s32[1]{0:T(128)} %bitcast.plane_ref, f32[832,512]{1,0:T(8,128)S(1)} %get-tuple-element.9.carried_ref, f32[128,128]{1,0:T(8,128)S(1)} %bitcast.19, f32[128,128]{1,0:T(8,128)S(1)} %collective-permute-done.f1_ref, f32[128,128]{1,0:T(8,128)S(1)} %collective-permute-done.1.f2_ref, ...), custom_call_target="tpu_custom_call" | custom-call | flops 68719476736 | bytes 16777216 | tf_op jit(solution)/shard_map/back_part/pallas_call | solution.py:331
  64.9 0.0 collective-permute-done.3.l1_ref
  64.9 0.0 collective-permute-done.4.l2_ref
  64.9 0.0 collective-permute-done.5.l3_ref
  64.9 1.5 %finish.1 = f32[1280,128]{1,0:T(8,128)} custom-call(f32[520,512]{1,0:T(8,128)S(1)} %back_part.1.back, f32[128,128]{1,0:T(8,128)S(1)} %get-tuple-element.17.l0_ref, f32[128,128]{1,0:T(8,128)S(1)} %collective-permute-done.3.l1_ref, f32[128,128]{1,0:T(8,128)S(1)} %collective-permute-done.4.l2_ref, f32[128,128]{1,0:T(8,128)S(1)} %collective-permute-done.5.l3_ref, ...), custom_call_target="tpu_custom_call" | custom-call | flops 268435456 | bytes 4194304 | tf_op jit(solution)/shard_map/finish/pallas_call | solution.py:347
  66.4 8.2 %all-to-all-start.1 = ((f32[64,5,4,128]{3,2,1,0:T(4,128)}), f32[64,5,4,128]{3,2,1,0:T(4,128)S(1)}, u32[]{:S(2)}, u32[]{:S(2)}) async-start(f32[64,5,4,128]{3,2,1,0:T(4,128)} %bitcast.8), calls=%async_computation.1 | async-start | bytes 1310720 | tf_op jit(solution)/shard_map/all_to_all | solution.py:377
  74.6 0.8 multiply_convert_fusion
  75.4 19.6 %all-to-all-done.1 = f32[64,5,4,128]{3,2,1,0:T(4,128)S(1)} async-done(((f32[64,5,4,128]{3,2,1,0:T(4,128)}), f32[64,5,4,128]{3,2,1,0:T(4,128)S(1)}, u32[]{:S(2)}, u32[]{:S(2)}) %all-to-all-start.1) | async-done | bytes 655392 | tf_op jit(solution)/shard_map/all_to_all | solution.py:377
  94.9 1.1 %unpack.1 = (bf16[256,512]{1,0:T(8,128)(2,1)}, bf16[256,512]{1,0:T(8,128)(2,1)}, f32[256,128]{1,0:T(8,128)}) custom-call(f32[1280,128]{1,0:T(8,128)S(1)} %bitcast.14, bf16[256,512]{1,0:T(8,128)(2,1)S(1)} %copy-done, bf16[256,512]{1,0:T(8,128)(2,1)S(1)} %copy-done.1), custom_call_target="tpu_custom_call" | custom-call | flops 1048576 | bytes 3145728 | tf_op jit(solution)/shard_map/unpack/pallas_call | solution.py:360
  (13 shorter events, 0.1 us)
Async XLA Ops:
  3.4 48.8 %copy-start.2 = (bf16[1536,256]{1,0:T(8,128)(2,1)S(1)}, bf16[1536,256]{1,0:T(8,128)(2,1)}, u32[]{:S(2)}) copy-start(bf16[1536,256]{1,0:T(8,128)(2,1)} %constant.9.clone.inv_ref) | copy-start | bytes 2359300
  3.4 48.8 %copy-start.3 = (s32[8]{0:T(128)S(1)}, s32[8]{0:T(128)}, u32[]{:S(2)}) copy-start(s32[8]{0:T(128)} %genome_ref.3) | copy-start | bytes 100
  3.4 48.8 %copy-start.4 = (bf16[768,512]{1,0:T(8,128)(2,1)S(1)}, bf16[768,512]{1,0:T(8,128)(2,1)}, u32[]{:S(2)}) copy-start(bf16[768,512]{1,0:T(8,128)(2,1)} %constant.8.clone.fwd_ref) | copy-start | bytes 2359300
  47.4 12.0 %collective-permute-start = (f32[128,128]{1,0:T(8,128)S(1)}, f32[128,128]{1,0:T(8,128)S(1)}, u32[]{:S(2)}, u32[]{:S(2)}) collective-permute-start(f32[128,128]{1,0:T(8,128)S(1)} %bitcast.16), channel_id=1, source_target_pairs={{0,1},{1,2},{2,3},{3,0},{4,5},{5,6},{6,7},{7,4},{8,9},{9,10},{10,1... | collective-permute-start | bytes 196616 | tf_op jit(solution)/shard_map/ppermute | solution.py:373
  48.7 12.3 %collective-permute-start.1 = (f32[128,128]{1,0:T(8,128)S(1)}, f32[128,128]{1,0:T(8,128)S(1)}, u32[]{:S(2)}, u32[]{:S(2)}) collective-permute-start(f32[128,128]{1,0:T(8,128)S(1)} %bitcast.17), channel_id=1, source_target_pairs={{0,2},{1,3},{2,0},{3,1},{4,6},{5,7},{6,4},{7,5},{8,10},{9,11},{10,... | collective-permute-start | bytes 196616 | tf_op jit(solution)/shard_map/ppermute | solution.py:373
  51.1 9.9 %collective-permute-start.2 = (f32[128,128]{1,0:T(8,128)S(1)}, f32[128,128]{1,0:T(8,128)S(1)}, u32[]{:S(2)}, u32[]{:S(2)}) collective-permute-start(f32[128,128]{1,0:T(8,128)S(1)} %bitcast.18), channel_id=1, source_target_pairs={{0,3},{1,0},{2,1},{3,2},{4,7},{5,4},{6,5},{7,6},{8,11},{9,8},{10,9... | collective-permute-start | bytes 196616 | tf_op jit(solution)/shard_map/ppermute | solution.py:373
  58.1 6.8 %collective-permute-start.3 = (f32[128,128]{1,0:T(8,128)S(1)}, f32[128,128]{1,0:T(8,128)S(1)}, u32[]{:S(2)}, u32[]{:S(2)}) collective-permute-start(f32[128,128]{1,0:T(8,128)S(1)} %get-tuple-element.16), channel_id=1, source_target_pairs={{0,1},{1,2},{2,3},{3,0},{4,5},{5,6},{6,7},{7,4},{8,9},{9,10},{10,1... | collective-permute-start | bytes 196616 | tf_op jit(solution)/shard_map/ppermute | solution.py:373
  58.5 6.4 %collective-permute-start.4 = (f32[128,128]{1,0:T(8,128)S(1)}, f32[128,128]{1,0:T(8,128)S(1)}, u32[]{:S(2)}, u32[]{:S(2)}) collective-permute-start(f32[128,128]{1,0:T(8,128)S(1)} %get-tuple-element.15), channel_id=1, source_target_pairs={{0,2},{1,3},{2,0},{3,1},{4,6},{5,7},{6,4},{7,5},{8,10},{9,11},{10,... | collective-permute-start | bytes 196616 | tf_op jit(solution)/shard_map/ppermute | solution.py:373
  59.4 5.6 %collective-permute-start.5 = (f32[128,128]{1,0:T(8,128)S(1)}, f32[128,128]{1,0:T(8,128)S(1)}, u32[]{:S(2)}, u32[]{:S(2)}) collective-permute-start(f32[128,128]{1,0:T(8,128)S(1)} %get-tuple-element.14), channel_id=1, source_target_pairs={{0,3},{1,0},{2,1},{3,2},{4,7},{5,4},{6,5},{7,6},{8,11},{9,8},{10,9... | collective-permute-start | bytes 196616 | tf_op jit(solution)/shard_map/ppermute | solution.py:373
  66.4 8.2 %copy-start.5 = (bf16[256,512]{1,0:T(8,128)(2,1)S(1)}, bf16[256,512]{1,0:T(8,128)(2,1)}, u32[]{:S(2)}) copy-start(bf16[256,512]{1,0:T(8,128)(2,1)} %g_hbm.1) | copy-start | bytes 786436
  66.4 8.2 %copy-start.6 = (bf16[256,512]{1,0:T(8,128)(2,1)S(1)}, bf16[256,512]{1,0:T(8,128)(2,1)}, u32[]{:S(2)}) copy-start(bf16[256,512]{1,0:T(8,128)(2,1)} %param.13) | copy-start | bytes 786436
  66.4 28.6 %copy-start = (bf16[256,512]{1,0:T(8,128)(2,1)S(1)}, bf16[256,512]{1,0:T(8,128)(2,1)}, u32[]{:S(2)}) copy-start(bf16[256,512]{1,0:T(8,128)(2,1)} %q_ref.1) | copy-start | bytes 786436
  66.4 28.6 %copy-start.1 = (bf16[256,512]{1,0:T(8,128)(2,1)S(1)}, bf16[256,512]{1,0:T(8,128)(2,1)}, u32[]{:S(2)}) copy-start(bf16[256,512]{1,0:T(8,128)(2,1)} %k_ref.1) | copy-start | bytes 786436
  66.4 28.5 %all-to-all-start.1 = ((f32[64,5,4,128]{3,2,1,0:T(4,128)}), f32[64,5,4,128]{3,2,1,0:T(4,128)S(1)}, u32[]{:S(2)}, u32[]{:S(2)}) async-start(f32[64,5,4,128]{3,2,1,0:T(4,128)} %bitcast.8), calls=%async_computation.1 | async-start | bytes 1310720 | tf_op jit(solution)/shard_map/all_to_all | solution.py:377

commit v2 on v1

v2 whole, which is shorter than its diff:
```python
import functools

import jax
import jax.numpy as jnp
import ml_dtypes
import numpy as np
from jax import lax
from jax.experimental import pallas as pl
from jax.experimental.pallas import tpu as pltpu
from jax.sharding import PartitionSpec as P

BLOCK = 256
LANES = 128
OWN = 8
PLANES = 4
NCTX = 64
MOST = 32
GENOMES = 8
UNROLL = 4
TILE = 4
GAP = UNROLL + TILE - 2
WIDE = 3 * BLOCK
IN_ROWS = 36
OUT_ROWS = 20
F32 = jnp.float32
BF16 = jnp.bfloat16


def split_table(table):
    high = table.astype(ml_dtypes.bfloat16)
    low = (table - high.astype(np.float64)).astype(ml_dtypes.bfloat16)
    return np.concatenate([high, low, high], axis=0)


def dft_tables():
    freq = np.arange(BLOCK)
    sample = np.arange(BLOCK)
    phase = (sample[:, None] * (2 * freq[None, :] + 1)) % (4 * BLOCK)
    angle = phase * (np.pi / (2 * BLOCK))
    forward = np.concatenate([np.cos(angle), -np.sin(angle)], axis=1)
    return split_table(forward), split_table(forward.T / BLOCK)


def dot3(x, table):
    high = x.astype(BF16)
    low = (x - high.astype(F32)).astype(BF16)
    return jnp.dot(
        jnp.concatenate([low, high, high], 1), table[...], preferred_element_type=F32
    )


def pack_kernel(
    plane_ref, q_hbm, k_hbm, v_hbm, g_hbm, f_hbm, out_ref, q_ref, k_ref, v_ref, g_ref, f_ref,
    turned, sems,
):
    column = pl.multiple_of(plane_ref[0] * LANES, LANES)
    pairs = (
        (g_hbm, g_ref), (v_hbm, v_ref), (q_hbm, q_ref), (k_hbm, k_ref),
        (f_hbm.at[:, pl.ds(column, LANES)], f_ref),
    )
    copies = [pltpu.make_async_copy(a, b, sems.at[i]) for i, (a, b) in enumerate(pairs)]
    for copy in copies:
        copy.start()

    for which, (a_ref, b_ref, first_copy) in enumerate(((g_ref, v_ref, 0), (q_ref, k_ref, 2))):
        copies[first_copy].wait()
        copies[first_copy + 1].wait()
        product = a_ref[...].astype(F32) * b_ref[...].astype(F32)
        for half in range(2):
            turned[half] = product[half * LANES : (half + 1) * LANES, :].T
        for half in range(2):
            for quarter in range(PLANES):
                for r in range(2):
                    rows = turned[half, pl.ds(LANES * quarter + r, NCTX, stride=2), :]
                    first = 16 * (1 - which) + 8 * half + 2 * quarter + r
                    out_ref[pl.ds(first, NCTX, stride=IN_ROWS), :] = rows
    copies[4].wait()
    for half in range(2):
        turned[half, 0:LANES, :] = f_ref[half * LANES : (half + 1) * LANES, :].T
        for r in range(2):
            rows = turned[half, pl.ds(r, NCTX, stride=2), :]
            out_ref[pl.ds(32 + 2 * half + r, NCTX, stride=IN_ROWS), :] = rows


def signs():
    lane = lax.broadcasted_iota(jnp.int32, (1, BLOCK), 1)
    return (1 - 2 * (lane % 2)).astype(F32)


def add_pairs(totals, pairs, first, second):
    for half in range(2):
        loaded = {}

        def load(name, view, index):
            if (name, index) not in loaded:
                loaded[name, index] = [
                    view[index, :, pl.ds(BLOCK * i + LANES * half, LANES)] for i in range(3)
                ]
            return loaded[name, index]

        out = {}
        for j, index, other in pairs:
            a, b = load("first", first, index), load("second", second, other)
            for i in range(3):
                lanes = pl.ds(BLOCK * i + LANES * half, LANES)
                if (j, i) not in out:
                    out[j, i] = totals[j, :, lanes]
                out[j, i] = out[j, i] + a[i] * b[i]
        for (j, i), value in out.items():
            totals[j, :, pl.ds(BLOCK * i + LANES * half, LANES)] = value


def lag_kernel(
    genome_ref, plane_ref, x_ref, fwd_ref, inv_ref, g_ref, c_ref,
    lag_ref, carried_ref, value_hbm, gated, lags, flat, value_ref, sem,
):
    value_ref[...] = (g_ref[...].astype(F32) * c_ref[...].astype(F32)).astype(BF16)
    give = pltpu.make_async_copy(value_ref, value_hbm, sem)
    give.start()
    end = jnp.int32(0)
    for g in range(GENOMES):
        end = end + genome_ref[g]
        carried_ref[pl.ds(end + GAP * g, GAP)] = jnp.zeros((GAP, OWN, WIDE), F32)
    lags[...] = jnp.zeros_like(lags)
    gated[NCTX:] = jnp.zeros((UNROLL, OWN, WIDE), F32)
    places, own, end = [], jnp.int32(0), genome_ref[0]
    for s in range(NCTX):
        if s:
            own = own + (s >= end).astype(jnp.int32)
            end = jnp.where(s >= end, end + genome_ref[own], end)
        places.append(s + GAP * own)
    group = 32
    for part in range(NCTX // group):
        for which in range(2):
            rows = []
            for s in range(part * group, (part + 1) * group):
                base = IN_ROWS * s + 16 * which
                rows.append(
                    jnp.concatenate([x_ref[base : base + 8, :], x_ref[base + 8 : base + 16, :]], 1)
                )
            spec = dot3(jnp.concatenate(rows, 0), fwd_ref).reshape(group, OWN, 2 * BLOCK)
            re, im = spec[:, :, :BLOCK], spec[:, :, BLOCK:]
            if which == 0:
                blocks = pl.ds(group * part, group)
                gated[blocks, :, 0:BLOCK] = re - im
                gated[blocks, :, BLOCK : 2 * BLOCK] = re
                gated[blocks, :, 2 * BLOCK : WIDE] = im
            else:
                less, more = im - re, re + im
                for i in range(group):
                    block = places[part * group + i]
                    carried_ref[block, :, 0:BLOCK] = re[i]
                    carried_ref[block, :, BLOCK : 2 * BLOCK] = less[i]
                    carried_ref[block, :, 2 * BLOCK : WIDE] = more[i]
    pairs = [(j, u, u + j) for u in range(UNROLL) for j in range(TILE)]

    def genome(g, begin):
        count = genome_ref[g]
        first = begin + GAP * g

        def tile(i, _):
            d = TILE * i

            totals = lags.at[pl.ds(d, TILE)]

            def step(c, _):
                s = UNROLL * c
                here = gated.at[pl.ds(begin + s, UNROLL)]
                after = carried_ref.at[pl.ds(first + d + s, UNROLL + TILE - 1)]
                add_pairs(totals, pairs, here, after)
                return 0

            lax.fori_loop(0, (count - d + UNROLL - 1) // UNROLL, step, 0)
            return 0

        lax.fori_loop(0, (count + TILE - 1) // TILE, tile, 0)
        return begin + count

    lax.fori_loop(0, GENOMES, genome, jnp.int32(0))
    sign = signs()
    k1, k2, k3 = [
        lags[: MOST + 1, :, BLOCK * i : BLOCK * (i + 1)].reshape(OWN * (MOST + 1), BLOCK)
        for i in range(3)
    ]
    re, im = k1 + k3, k1 + k2
    spec = jnp.concatenate(
        [re[: OWN * MOST] + sign * im[OWN:], im[: OWN * MOST] - sign * re[OWN:]], 1
    )
    rows = dot3(spec, inv_ref)
    for half in range(2):
        flat[half] = rows[:, half * LANES : (half + 1) * LANES]
    for quarter in range(PLANES):
        slot = lax.bitwise_xor(jnp.int32(quarter), plane_ref[0])
        for half in range(2):
            for r in range(2):
                rows = flat[half, pl.ds(2 * quarter + r, MOST, stride=OWN), :]
                lag_ref[slot, pl.ds(2 * half + r, MOST, stride=4), :] = rows
    give.wait()


def back_kernel(
    genome_ref, plane_ref, carried_ref, f0_ref, f1_ref, f2_ref, f3_ref, fwd_ref, back, filt, flat,
):
    for k, f_ref in enumerate((f0_ref, f1_ref, f2_ref, f3_ref)):
        quarter = lax.bitwise_xor(jnp.int32(k), plane_ref[0])
        for half in range(2):
            for r in range(2):
                rows = f_ref[pl.ds(2 * half + r, MOST, stride=4), :]
                flat[half, pl.ds(2 * quarter + r, MOST, stride=OWN), :] = rows
    spec = dot3(jnp.concatenate([flat[0], flat[1]], 1), fwd_ref)
    sign = signs()
    prior = jnp.concatenate([jnp.zeros((OWN, 2 * BLOCK), F32), spec[: OWN * (MOST - 1), :]], 0)
    re = spec[:, :BLOCK] - sign * prior[:, BLOCK:]
    im = spec[:, BLOCK:] + sign * prior[:, :BLOCK]
    head = TILE - 1
    filt[:head] = jnp.zeros((head, OWN, WIDE), F32)
    for i, value in enumerate((re - im, re, im)):
        filt[head : head + MOST, :, BLOCK * i : BLOCK * (i + 1)] = value.reshape(MOST, OWN, BLOCK)
    filt[head + MOST :] = jnp.zeros((UNROLL, OWN, WIDE), F32)
    pairs = [(j, u - j + head, u) for u in range(UNROLL) for j in range(TILE)]

    def genome(g, begin):
        count = genome_ref[g]
        first = begin + GAP * g

        def tile(i, _):
            b = TILE * i

            totals = back.at[pl.ds(begin + b, TILE)]
            totals[...] = jnp.zeros((TILE, OWN, WIDE), F32)

            def step(c, _):
                t = UNROLL * c
                taps = filt.at[pl.ds(t, UNROLL + TILE - 1)]
                later = carried_ref.at[pl.ds(first + b + t, UNROLL)]
                add_pairs(totals, pairs, taps, later)
                return 0

            lax.fori_loop(0, (count - b + UNROLL - 1) // UNROLL, step, 0)
            return 0

        lax.fori_loop(0, (count + TILE - 1) // TILE, tile, 0)
        return begin + count

    lax.fori_loop(0, GENOMES, genome, jnp.int32(0))


def finish_kernel(back, l0_ref, l1_ref, l2_ref, l3_ref, inv_ref, out_ref):
    group = 32
    for part in range(NCTX // group):
        k1, k2, k3 = [
            back[group * part : group * (part + 1), :, BLOCK * i : BLOCK * (i + 1)].reshape(
                OWN * group, BLOCK
            )
            for i in range(3)
        ]
        rows = dot3(jnp.concatenate([k1 + k3, k1 + k2], 1), inv_ref)
        for i in range(group):
            base = OUT_ROWS * (part * group + i)
            for half in range(2):
                out_ref[base + 8 * half : base + 8 * half + 8, :] = rows[
                    OWN * i : OWN * (i + 1), half * LANES : (half + 1) * LANES
                ]
    for i in range(MOST):
        part = slice(4 * i, 4 * i + 4)
        total = (l0_ref[part, :] + l1_ref[part, :]) + (l2_ref[part, :] + l3_ref[part, :])
        out_ref[OUT_ROWS * i + 16 : OUT_ROWS * i + 20, :] = total
    for i in range(MOST, NCTX):
        out_ref[OUT_ROWS * i + 16 : OUT_ROWS * i + 20, :] = jnp.zeros((4, LANES), F32)


def unpack_kernel(
    scale, x_ref, q_ref, k_ref, gq_hbm, gk_hbm, gf_hbm, gq_ref, gk_ref, gf_ref, turned, sems
):
    copies = []

    def send(source, target, rows):
        copy = pltpu.make_async_copy(source.at[rows], target.at[rows], sems.at[len(copies)])
        copy.start()
        copies.append(copy)

    for half in range(2):
        for quarter in range(PLANES):
            for r in range(2):
                rows = x_ref[pl.ds(8 * half + 2 * quarter + r, NCTX, stride=OUT_ROWS), :]
                turned[half, pl.ds(LANES * quarter + r, NCTX, stride=2), :] = rows
        part = pl.ds(half * LANES, LANES)
        back = turned[half].T
        gq_ref[part, :] = (back * k_ref[part, :].astype(F32)).astype(BF16)
        send(gq_ref, gq_hbm, part)
        gk_ref[part, :] = (back * q_ref[part, :].astype(F32)).astype(BF16)
        send(gk_ref, gk_hbm, part)
        for r in range(2):
            rows = x_ref[pl.ds(16 + 2 * half + r, NCTX, stride=OUT_ROWS), :]
            turned[half, pl.ds(r, NCTX, stride=2), :] = rows
        gf_ref[part, :] = turned[half, 0:LANES, :].T * scale
        send(gf_ref, gf_hbm, part)
    for copy in copies:
        copy.wait()


VMEM = pl.BlockSpec(memory_space=pltpu.VMEM)
SMEM = pl.BlockSpec(memory_space=pltpu.SMEM)
HBM = pl.BlockSpec(memory_space=pltpu.HBM)


def params(mib=40):
    return pltpu.CompilerParams(vmem_limit_bytes=mib * 1024 * 1024)


def cost(flops, moved):
    return pl.CostEstimate(flops=flops, bytes_accessed=moved, transcendentals=0)


def shape(*dims):
    return jax.ShapeDtypeStruct(dims, F32)


def in_hbm(*arrays):
    return [pltpu.with_memory_space_constraint(a, pltpu.HBM) for a in arrays]


def pack(plane, q, k, v, g, f):
    half = pltpu.VMEM(q.shape, BF16)
    return pl.pallas_call(
        pack_kernel,
        out_shape=pltpu.VMEM((NCTX * IN_ROWS, LANES), F32),
        in_specs=[SMEM] + [HBM] * 5,
        out_specs=VMEM,
        scratch_shapes=[half] * 4
        + [
            pltpu.VMEM((BLOCK, LANES), F32),
            pltpu.VMEM((2, 2 * BLOCK, LANES), F32),
            pltpu.SemaphoreType.DMA((5,)),
        ],
        compiler_params=params(),
        cost_estimate=cost(1 << 20, 3 << 20),
        name="pack",
    )(plane, *in_hbm(q, k, v, g, f))


def lag_part(genome_blocks, plane, x, tables, g, c):
    return pl.pallas_call(
        lag_kernel,
        out_shape=[
            shape(PLANES, 4 * MOST, LANES),
            shape(NCTX + GAP * GENOMES, OWN, WIDE),
            pltpu.HBM(g.shape, BF16),
        ],
        in_specs=[SMEM] * 2 + [VMEM] * 5,
        out_specs=[VMEM, VMEM, HBM],
        scratch_shapes=[
            pltpu.VMEM((NCTX + UNROLL, OWN, WIDE), F32),
            pltpu.VMEM((MOST + TILE, OWN, WIDE), F32),
            pltpu.VMEM((2, OWN * MOST, LANES), F32),
            pltpu.VMEM(g.shape, BF16),
            pltpu.SemaphoreType.DMA(()),
        ],
        compiler_params=params(),
        cost_estimate=cost(1 << 36, 16 << 20),
        name="lag_part",
    )(genome_blocks, plane, x, *tables, g, c)


def back_part(genome_blocks, plane, carried, quarters, table):
    return pl.pallas_call(
        back_kernel,
        out_shape=shape(NCTX + TILE, OWN, WIDE),
        in_specs=[SMEM, SMEM] + [VMEM] * 6,
        out_specs=VMEM,
        scratch_shapes=[
            pltpu.VMEM((TILE - 1 + MOST + UNROLL, OWN, WIDE), F32),
            pltpu.VMEM((2, OWN * MOST, LANES), F32),
        ],
        compiler_params=params(),
        cost_estimate=cost(1 << 36, 16 << 20),
        name="back_part",
    )(genome_blocks, plane, carried, *quarters, table)


def finish(back, lags, table):
    return pl.pallas_call(
        finish_kernel,
        out_shape=pltpu.VMEM((NCTX * OUT_ROWS, LANES), F32),
        in_specs=[VMEM] * 6,
        out_specs=VMEM,
        compiler_params=params(),
        cost_estimate=cost(1 << 28, 4 << 20),
        name="finish",
    )(back, *lags, table)


def unpack(x, q, k, scale):
    half = pltpu.VMEM(q.shape, BF16)
    wide = pltpu.VMEM((BLOCK, LANES), F32)
    return pl.pallas_call(
        functools.partial(unpack_kernel, scale),
        out_shape=[pltpu.HBM(a.shape, a.dtype) for a in (half, half, wide)],
        in_specs=[VMEM] * 3,
        out_specs=[HBM] * 3,
        scratch_shapes=[
            half,
            half,
            wide,
            pltpu.VMEM((2, 2 * BLOCK, LANES), F32),
            pltpu.SemaphoreType.DMA((6,)),
        ],
        compiler_params=params(),
        cost_estimate=cost(1 << 20, 3 << 20),
        name="unpack",
    )(x, q, k)


def shift(x, k):
    return lax.ppermute(x, "ch", [(i, i ^ k) for i in range(PLANES)])


def exchange(x):
    return lax.all_to_all(x, "ctx", split_axis=0, concat_axis=0, tiled=True)


def local(q, k, v, g, c, filters, genome_blocks):
    forward, inverse = [jnp.asarray(t) for t in dft_tables()]
    plane = lax.axis_index("ch").astype(jnp.int32).reshape(1)
    sent = pack(plane, q, k, v, g, filters)
    got = exchange(sent.reshape(NCTX, IN_ROWS // 4, 4, LANES))
    own_quarter = got[:MOST, 8].reshape(4 * MOST, LANES)
    quarters = [own_quarter] + [shift(own_quarter, i) for i in range(1, PLANES)]
    slots, carried, grad_value = lag_part(
        genome_blocks, plane, got.reshape(NCTX * IN_ROWS, LANES), (forward, inverse), g, c
    )
    lags = [slots[0]] + [shift(slots[i], i) for i in range(1, PLANES)]
    back = back_part(genome_blocks, plane, carried, quarters, forward)
    out = finish(back, lags, inverse).reshape(NCTX, OUT_ROWS // 4, 4, LANES)
    returned = exchange(out).reshape(NCTX * OUT_ROWS, LANES)
    scale = (NCTX * BLOCK) ** (-0.5)
    grad_query, grad_key, grad_filters = unpack(returned, q, k, scale)
    return grad_query, grad_key, grad_value, grad_filters


def solution(mesh):
    split = P("ctx", "ch")
    return jax.shard_map(
        local,
        mesh=mesh,
        in_specs=(split,) * 5 + (P("ctx", None), P()),
        out_specs=(split,) * 4,
        check_vma=False,
    )
```

time: 96.3 us -> 92.4 us (0.960)
  blocking collectives: 43.9 us -> 72.7 us
  waiting for transfers between devices: 19.6 us -> 0.73 us
  starting transfers between devices: 15.9 us -> 6.68 us
  Pallas kernels: 15 us -> 11.3 us
    all_to_all x1 -> x2, blocking collectives: 43.9 us -> 72.7 us  [exchange(): return lax.all_to_all(x, 'ctx', split_axis=0, concat_axis=0, tiled=True)]
    all_to_all x1 -> x0, waiting for transfers between devices: 19.6 us -> none  [exchange(): return lax.all_to_all(x, 'ctx', split_axis=0, concat_axis=0, tiled=True)]
    all_to_all x1 -> x0, starting transfers between devices: 8.17 us -> none  [exchange(): return lax.all_to_all(x, 'ctx', split_axis=0, concat_axis=0, tiled=True)]
    pallas_call x4, Pallas kernels: 9.2 us -> 6.51 us  [the longest x1 3.16 us: back_part(): pl.pallas_call(back_kernel, out_shape=shape(NCTX + TILE, OWN, WIDE), in_s...]
    ppermute x6, starting transfers between devices: 7.77 us -> 6.68 us  [shift(): return lax.ppermute(x, 'ch', [(i, i ^ k) for i in range(PLANES)])]
  transfers between devices with their start and end apart: 7 -> 6, of which waited for: 1 -> 1; matrix products, arithmetic and copies ran while one was open for 1% -> 0% of each run, Pallas kernels for 10% -> 9%
where the time goes in v2:
time: 92.4 us; the launch traced here: 92.3 us
  blocking collectives  72.7 us (79%)
  Pallas kernels  11.3 us (12%)
  starting transfers between devices  6.68 us (7%)
    all_to_all x2, blocking collectives, exchange(): return lax.all_to_all(x, 'ctx', split_axis=0, concat_axis=0, tiled=True)  72.7 us
    ppermute x6, starting transfers between devices, shift(): return lax.ppermute(x, 'ch', [(i, i ^ k) for i in range(PLANES)])  6.68 us
    pallas_call x1, Pallas kernels, lag_part(): pl.pallas_call(lag_kernel, out_shape=[shape(PLANES, 4 * MOST, LANES), sha...  4.84 us
    pallas_call x1, Pallas kernels, back_part(): pl.pallas_call(back_kernel, out_shape=shape(NCTX + TILE, OWN, WIDE), in_s...  3.16 us
  transfers between devices with their start and end apart: 6, of which 1 were waited for; matrix products, arithmetic and copies ran while one was open for 0% of the time, Pallas kernels for 9%

profile of v2, /device:TPU:1, one launch (start us, length us, event | category | flops | bytes accessed | tf_op | source)
XLA Modules:
  0.0 92.3 jit_solution(6640042319506376954)
XLA Ops:
  0.6 1.7 %pack.1 = f32[2304,128]{1,0:T(8,128)S(1)} custom-call(s32[1]{0:T(128)} %bitcast.plane_ref, bf16[256,512]{1,0:T(8,128)(2,1)} %q_ref.1, bf16[256,512]{1,0:T(8,128)(2,1)} %k_ref.1, bf16[256,512]{1,0:T(8,128)(2,1)} %v_hbm.1, bf16[256,512]{1,0:T(8,128)(2,1)} %g_ref.1, f32[256,512]{1,0:T(8,128)} %f_hbm.1), custom_call_target="tpu_custom_call" | custom-call | flops 1048576 | bytes 3145728 | tf_op jit(solution)/shard_map/pack/pallas_call | solution.py:325
  2.4 0.0 copy-start.2
  2.4 0.0 copy-start.3
  2.4 0.0 copy-start.4
  2.4 0.0 copy-start.5
  2.4 0.0 copy-start.6
  2.4 43.7 %all_to_all.10 = f32[64,9,4,128]{3,2,1,0:T(4,128)S(1)} all-to-all(f32[64,9,4,128]{3,2,1,0:T(4,128)S(1)} %bitcast.14), channel_id=1, replica_groups=mesh['ctx'=64,'ch'=4] {'ctx'}, dimensions={0} | all-to-all | bytes 2359296 | tf_op jit(solution)/shard_map/all_to_all | solution.py:419
  46.1 2.6 %collective-permute-start.2 = (f32[128,128]{1,0:T(8,128)S(1)}, f32[128,128]{1,0:T(8,128)S(1)}, u32[]{:S(2)}, u32[]{:S(2)}) collective-permute-start(f32[128,128]{1,0:T(8,128)S(1)} %bitcast.18), channel_id=1, source_target_pairs={{0,3},{1,2},{2,1},{3,0},{4,7},{5,6},{6,5},{7,4},{8,11},{9,10},{10,... | collective-permute-start | bytes 196616 | tf_op jit(solution)/shard_map/ppermute | solution.py:415
  48.7 0.5 collective-permute-start.1
  49.2 0.3 collective-permute-start
  49.5 4.8 %lag_part.1 = (f32[4,128,128]{2,1,0:T(8,128)S(1)}, f32[112,8,768]{2,1,0:T(8,128)S(1)}, bf16[256,512]{1,0:T(8,128)(2,1)}) custom-call(s32[8]{0:T(128)S(1)} %copy-done.5, s32[1]{0:T(128)} %bitcast.plane_ref, f32[2304,128]{1,0:T(8,128)S(1)} %bitcast.17, bf16[768,512]{1,0:T(8,128)(2,1)S(1)} %copy-done.6, bf16[1536,256]{1,0:T(8,128)(2,1)S(1)} %copy-done.2, ...), custom_call_target="tpu_custom_call" | custom-call | flops 68719476736 | bytes 16777216 | tf_op jit(solution)/shard_map/lag_part/pallas_call | solution.py:343
  54.4 2.6 %collective-permute-start.5 = (f32[128,128]{1,0:T(8,128)S(1)}, f32[128,128]{1,0:T(8,128)S(1)}, u32[]{:S(2)}, u32[]{:S(2)}) collective-permute-start(f32[128,128]{1,0:T(8,128)S(1)} %get-tuple-element.16), channel_id=1, source_target_pairs={{0,3},{1,2},{2,1},{3,0},{4,7},{5,6},{6,5},{7,4},{8,11},{9,10},{10,... | collective-permute-start | bytes 196616 | tf_op jit(solution)/shard_map/ppermute | solution.py:415
  56.9 0.5 collective-permute-start.4
  57.5 0.0 collective-permute-done.2.f3_ref
  57.5 0.3 collective-permute-start.3
  57.7 0.0 collective-permute-done.1.f2_ref
  57.7 0.0 collective-permute-done.f1_ref
  57.7 3.2 %back_part.1.back = f32[68,8,768]{2,1,0:T(8,128)S(1)} custom-call(s32[8]{0:T(128)S(1)} %copy-done.5, s32[1]{0:T(128)} %bitcast.plane_ref, f32[112,8,768]{2,1,0:T(8,128)S(1)} %get-tuple-element.10.carried_ref, f32[128,128]{1,0:T(8,128)S(1)} %bitcast.21, f32[128,128]{1,0:T(8,128)S(1)} %collective-permute-done.f1_ref, ...), custom_call_target="tpu_custom_call" | custom-call | flops 68719476736 | bytes 16777216 | tf_op jit(solution)/shard_map/back_part/pallas_call | solution.py:366
  60.9 0.0 collective-permute-done.5.l3_ref
  60.9 0.7 collective-permute-done.4.l2_ref
  61.6 0.0 collective-permute-done.3.l1_ref
  61.6 0.6 finish.1
  62.2 29.0 %all_to_all.11 = f32[64,5,4,128]{3,2,1,0:T(4,128)S(1)} all-to-all(f32[64,5,4,128]{3,2,1,0:T(4,128)S(1)} %bitcast.15), channel_id=1, replica_groups=mesh['ctx'=64,'ch'=4] {'ctx'}, dimensions={0} | all-to-all | bytes 1310720 | tf_op jit(solution)/shard_map/all_to_all | solution.py:419
  91.2 1.0 %unpack.1 = (bf16[256,512]{1,0:T(8,128)(2,1)}, bf16[256,512]{1,0:T(8,128)(2,1)}, f32[256,128]{1,0:T(8,128)}) custom-call(f32[1280,128]{1,0:T(8,128)S(1)} %bitcast.16, bf16[256,512]{1,0:T(8,128)(2,1)S(1)} %copy-done, bf16[256,512]{1,0:T(8,128)(2,1)S(1)} %copy-done.1), custom_call_target="tpu_custom_call" | custom-call | flops 1048576 | bytes 3145728 | tf_op jit(solution)/shard_map/unpack/pallas_call | solution.py:396
  (11 shorter events, 0.1 us)
Async XLA Ops:
  2.4 47.1 %copy-start.2 = (bf16[1536,256]{1,0:T(8,128)(2,1)S(1)}, bf16[1536,256]{1,0:T(8,128)(2,1)}, u32[]{:S(2)}) copy-start(bf16[1536,256]{1,0:T(8,128)(2,1)} %constant.9.clone.inv_ref) | copy-start | bytes 2359300
  2.4 47.1 %copy-start.3 = (bf16[256,512]{1,0:T(8,128)(2,1)S(1)}, bf16[256,512]{1,0:T(8,128)(2,1)}, u32[]{:S(2)}) copy-start(bf16[256,512]{1,0:T(8,128)(2,1)} %g_ref.1) | copy-start | bytes 786436
  2.4 47.1 %copy-start.4 = (bf16[256,512]{1,0:T(8,128)(2,1)S(1)}, bf16[256,512]{1,0:T(8,128)(2,1)}, u32[]{:S(2)}) copy-start(bf16[256,512]{1,0:T(8,128)(2,1)} %c_ref.1) | copy-start | bytes 786436
  2.4 47.1 %copy-start.5 = (s32[8]{0:T(128)S(1)}, s32[8]{0:T(128)}, u32[]{:S(2)}) copy-start(s32[8]{0:T(128)} %genome_ref.3) | copy-start | bytes 100
  2.4 47.1 %copy-start.6 = (bf16[768,512]{1,0:T(8,128)(2,1)S(1)}, bf16[768,512]{1,0:T(8,128)(2,1)}, u32[]{:S(2)}) copy-start(bf16[768,512]{1,0:T(8,128)(2,1)} %constant.8.clone.fwd_ref) | copy-start | bytes 2359300
  46.1 11.3 %collective-permute-start.2 = (f32[128,128]{1,0:T(8,128)S(1)}, f32[128,128]{1,0:T(8,128)S(1)}, u32[]{:S(2)}, u32[]{:S(2)}) collective-permute-start(f32[128,128]{1,0:T(8,128)S(1)} %bitcast.18), channel_id=1, source_target_pairs={{0,3},{1,2},{2,1},{3,0},{4,7},{5,6},{6,5},{7,4},{8,11},{9,10},{10,... | collective-permute-start | bytes 196616 | tf_op jit(solution)/shard_map/ppermute | solution.py:415
  48.7 9.0 %collective-permute-start.1 = (f32[128,128]{1,0:T(8,128)S(1)}, f32[128,128]{1,0:T(8,128)S(1)}, u32[]{:S(2)}, u32[]{:S(2)}) collective-permute-start(f32[128,128]{1,0:T(8,128)S(1)} %bitcast.19), channel_id=1, source_target_pairs={{0,2},{1,3},{2,0},{3,1},{4,6},{5,7},{6,4},{7,5},{8,10},{9,11},{10,... | collective-permute-start | bytes 196616 | tf_op jit(solution)/shard_map/ppermute | solution.py:415
  49.2 8.5 %collective-permute-start = (f32[128,128]{1,0:T(8,128)S(1)}, f32[128,128]{1,0:T(8,128)S(1)}, u32[]{:S(2)}, u32[]{:S(2)}) collective-permute-start(f32[128,128]{1,0:T(8,128)S(1)} %bitcast.20), channel_id=1, source_target_pairs={{0,1},{1,0},{2,3},{3,2},{4,5},{5,4},{6,7},{7,6},{8,9},{9,8},{10,11... | collective-permute-start | bytes 196616 | tf_op jit(solution)/shard_map/ppermute | solution.py:415
  54.4 6.5 %collective-permute-start.5 = (f32[128,128]{1,0:T(8,128)S(1)}, f32[128,128]{1,0:T(8,128)S(1)}, u32[]{:S(2)}, u32[]{:S(2)}) collective-permute-start(f32[128,128]{1,0:T(8,128)S(1)} %get-tuple-element.16), channel_id=1, source_target_pairs={{0,3},{1,2},{2,1},{3,0},{4,7},{5,6},{6,5},{7,4},{8,11},{9,10},{10,... | collective-permute-start | bytes 196616 | tf_op jit(solution)/shard_map/ppermute | solution.py:415
  56.9 4.7 %collective-permute-start.4 = (f32[128,128]{1,0:T(8,128)S(1)}, f32[128,128]{1,0:T(8,128)S(1)}, u32[]{:S(2)}, u32[]{:S(2)}) collective-permute-start(f32[128,128]{1,0:T(8,128)S(1)} %get-tuple-element.17), channel_id=1, source_target_pairs={{0,2},{1,3},{2,0},{3,1},{4,6},{5,7},{6,4},{7,5},{8,10},{9,11},{10,... | collective-permute-start | bytes 196616 | tf_op jit(solution)/shard_map/ppermute | solution.py:415
  57.5 4.2 %collective-permute-start.3 = (f32[128,128]{1,0:T(8,128)S(1)}, f32[128,128]{1,0:T(8,128)S(1)}, u32[]{:S(2)}, u32[]{:S(2)}) collective-permute-start(f32[128,128]{1,0:T(8,128)S(1)} %get-tuple-element.18), channel_id=1, source_target_pairs={{0,1},{1,0},{2,3},{3,2},{4,5},{5,4},{6,7},{7,6},{8,9},{9,8},{10,11... | collective-permute-start | bytes 196616 | tf_op jit(solution)/shard_map/ppermute | solution.py:415
  61.6 29.6 %copy-start = (bf16[256,512]{1,0:T(8,128)(2,1)S(1)}, bf16[256,512]{1,0:T(8,128)(2,1)}, u32[]{:S(2)}) copy-start(bf16[256,512]{1,0:T(8,128)(2,1)} %q_ref.1) | copy-start | bytes 786436
  61.6 29.6 %copy-start.1 = (bf16[256,512]{1,0:T(8,128)(2,1)S(1)}, bf16[256,512]{1,0:T(8,128)(2,1)}, u32[]{:S(2)}) copy-start(bf16[256,512]{1,0:T(8,128)(2,1)} %k_ref.1) | copy-start | bytes 786436

commit v3 on v2

--- a/solution.py
+++ b/solution.py
@@ -44,9 +44,12 @@
 def dot3(x, table):
     high = x.astype(BF16)
     low = (x - high.astype(F32)).astype(BF16)
-    return jnp.dot(
-        jnp.concatenate([low, high, high], 1), table[...], preferred_element_type=F32
-    )
+    left = jnp.concatenate([low, high, high], 1)
+    parts = [
+        jnp.dot(left, table[:, i : i + BLOCK], preferred_element_type=F32)
+        for i in range(0, table.shape[1], BLOCK)
+    ]
+    return jnp.concatenate(parts, 1) if len(parts) > 1 else parts[0]
 
 
 def pack_kernel(
@@ -59,9 +62,15 @@
         (f_hbm.at[:, pl.ds(column, LANES)], f_ref),
     )
     copies = [pltpu.make_async_copy(a, b, sems.at[i]) for i, (a, b) in enumerate(pairs)]
-    for copy in copies:
+    for copy in copies[4:] + copies[:4]:
         copy.start()
 
+    copies[4].wait()
+    for half in range(2):
+        turned[half, 0:LANES, :] = f_ref[half * LANES : (half + 1) * LANES, :].T
+        for r in range(2):
+            rows = turned[half, pl.ds(r, NCTX, stride=2), :]
+            out_ref[pl.ds(32 + 2 * half + r, NCTX, stride=IN_ROWS), :] = rows
     for which, (a_ref, b_ref, first_copy) in enumerate(((g_ref, v_ref, 0), (q_ref, k_ref, 2))):
         copies[first_copy].wait()
         copies[first_copy + 1].wait()
@@ -74,12 +83,6 @@
                     rows = turned[half, pl.ds(LANES * quarter + r, NCTX, stride=2), :]
                     first = 16 * (1 - which) + 8 * half + 2 * quarter + r
                     out_ref[pl.ds(first, NCTX, stride=IN_ROWS), :] = rows
-    copies[4].wait()
-    for half in range(2):
-        turned[half, 0:LANES, :] = f_ref[half * LANES : (half + 1) * LANES, :].T
-        for r in range(2):
-            rows = turned[half, pl.ds(r, NCTX, stride=2), :]
-            out_ref[pl.ds(32 + 2 * half + r, NCTX, stride=IN_ROWS), :] = rows
 
 
 def signs():
@@ -186,9 +189,13 @@
     spec = jnp.concatenate(
         [re[: OWN * MOST] + sign * im[OWN:], im[: OWN * MOST] - sign * re[OWN:]], 1
     )
-    rows = dot3(spec, inv_ref)
-    for half in range(2):
-        flat[half] = rows[:, half * LANES : (half + 1) * LANES]
+    for part in range(2):
+        top = OWN * MOST // 2 * part
+        rows = dot3(spec[top : top + OWN * MOST // 2, :], inv_ref)
+        for half in range(2):
+            flat[half, top : top + OWN * MOST // 2, :] = rows[
+                :, half * LANES : (half + 1) * LANES
+            ]
     for quarter in range(PLANES):
         slot = lax.bitwise_xor(jnp.int32(quarter), plane_ref[0])
         for half in range(2):
@@ -425,10 +432,12 @@
     sent = pack(plane, q, k, v, g, filters)
     got = exchange(sent.reshape(NCTX, IN_ROWS // 4, 4, LANES))
     own_quarter = got[:MOST, 8].reshape(4 * MOST, LANES)
-    quarters = [own_quarter] + [shift(own_quarter, i) for i in range(1, PLANES)]
+    near, other = shift(own_quarter, 1), shift(own_quarter, 3)
     slots, carried, grad_value = lag_part(
         genome_blocks, plane, got.reshape(NCTX * IN_ROWS, LANES), (forward, inverse), g, c
     )
+    slots, relayed = lax.optimization_barrier((slots, near))
+    quarters = [own_quarter, near, shift(relayed, 3), other]
     lags = [slots[0]] + [shift(slots[i], i) for i in range(1, PLANES)]
     back = back_part(genome_blocks, plane, carried, quarters, forward)
     out = finish(back, lags, inverse).reshape(NCTX, OUT_ROWS // 4, 4, LANES)

time: 92.4 us -> 91.4 us (0.989)
  transfers between devices with their start and end apart: 6 -> 6, of which waited for: 1 -> 1; matrix products, arithmetic and copies ran while one was open for 0% -> 0% of each run, Pallas kernels for 9% -> 8%
where the time goes in v3:
time: 91.4 us; the launch traced here: 91.3 us
  blocking collectives  72.6 us (79%)
  Pallas kernels  10.8 us (12%)
  starting transfers between devices  6.78 us (7%)
    all_to_all x2, blocking collectives, exchange(): return lax.all_to_all(x, 'ctx', split_axis=0, concat_axis=0, tiled=True)  72.6 us
    ppermute x6, starting transfers between devices, shift(): return lax.ppermute(x, 'ch', [(i, i ^ k) for i in range(PLANES)])  6.78 us
    pallas_call x1, Pallas kernels, lag_part(): pl.pallas_call(lag_kernel, out_shape=[shape(PLANES, 4 * MOST, LANES), sha...  4.33 us
    pallas_call x1, Pallas kernels, back_part(): pl.pallas_call(back_kernel, out_shape=shape(NCTX + TILE, OWN, WIDE), in_s...  3.15 us
  transfers between devices with their start and end apart: 6, of which 1 were waited for; matrix products, arithmetic and copies ran while one was open for 0% of the time, Pallas kernels for 8%

profile of v3, /device:TPU:1, one launch (start us, length us, event | category | flops | bytes accessed | tf_op | source)
XLA Modules:
  0.0 91.3 jit_solution(13190493346452639156)
XLA Ops:
  0.6 1.7 %pack.1 = f32[2304,128]{1,0:T(8,128)S(1)} custom-call(s32[1]{0:T(128)} %bitcast.plane_ref, bf16[256,512]{1,0:T(8,128)(2,1)} %q_ref.1, bf16[256,512]{1,0:T(8,128)(2,1)} %k_ref.1, bf16[256,512]{1,0:T(8,128)(2,1)} %v_hbm.1, bf16[256,512]{1,0:T(8,128)(2,1)} %g_ref.1, f32[256,512]{1,0:T(8,128)} %f_hbm.1), custom_call_target="tpu_custom_call" | custom-call | flops 1048576 | bytes 3145728 | tf_op jit(solution)/shard_map/pack/pallas_call | solution.py:332
  2.3 0.0 copy-start.2
  2.3 0.0 copy-start.3
  2.4 0.0 copy-start.4
  2.4 0.0 copy-start.5
  2.4 0.0 copy-start.6
  2.4 43.7 %all_to_all.10 = f32[64,9,4,128]{3,2,1,0:T(4,128)S(1)} all-to-all(f32[64,9,4,128]{3,2,1,0:T(4,128)S(1)} %bitcast.14), channel_id=1, replica_groups=mesh['ctx'=64,'ch'=4] {'ctx'}, dimensions={0} | all-to-all | bytes 2359296 | tf_op jit(solution)/shard_map/all_to_all | solution.py:426
  46.1 2.6 %collective-permute-start.2 = (f32[128,128]{1,0:T(8,128)S(1)}, f32[128,128]{1,0:T(8,128)S(1)}, u32[]{:S(2)}, u32[]{:S(2)}) collective-permute-start(f32[128,128]{1,0:T(8,128)S(1)} %bitcast.18), channel_id=1, source_target_pairs={{0,3},{1,2},{2,1},{3,0},{4,7},{5,6},{6,5},{7,4},{8,11},{9,10},{10,... | collective-permute-start | bytes 196616 | tf_op jit(solution)/shard_map/ppermute | solution.py:422
  48.7 0.0 collective-permute-start
  48.7 4.3 %lag_part.1 = (f32[4,128,128]{2,1,0:T(8,128)S(1)}, f32[112,8,768]{2,1,0:T(8,128)S(1)}, bf16[256,512]{1,0:T(8,128)(2,1)}) custom-call(s32[8]{0:T(128)S(1)} %copy-done.5, s32[1]{0:T(128)} %bitcast.plane_ref, f32[2304,128]{1,0:T(8,128)S(1)} %bitcast.17, bf16[768,512]{1,0:T(8,128)(2,1)S(1)} %copy-done.6, bf16[1536,256]{1,0:T(8,128)(2,1)S(1)} %copy-done.2, ...), custom_call_target="tpu_custom_call" | custom-call | flops 68719476736 | bytes 16777216 | tf_op jit(solution)/shard_map/lag_part/pallas_call | solution.py:350
  53.0 0.0 collective-permute-done.f1_ref
  53.0 0.9 collective-permute-start.1
  53.9 2.0 %collective-permute-start.5 = (f32[128,128]{1,0:T(8,128)S(1)}, f32[128,128]{1,0:T(8,128)S(1)}, u32[]{:S(2)}, u32[]{:S(2)}) collective-permute-start(f32[128,128]{1,0:T(8,128)S(1)} %get-tuple-element.20), channel_id=1, source_target_pairs={{0,3},{1,2},{2,1},{3,0},{4,7},{5,6},{6,5},{7,4},{8,11},{9,10},{10,... | collective-permute-start | bytes 196616 | tf_op jit(solution)/shard_map/ppermute | solution.py:422
  55.9 0.7 collective-permute-start.4
  56.6 0.7 collective-permute-start.3
  57.3 0.2 collective-permute-done.1.f2_ref
  57.5 3.2 %back_part.1.back = f32[68,8,768]{2,1,0:T(8,128)S(1)} custom-call(s32[8]{0:T(128)S(1)} %copy-done.5, s32[1]{0:T(128)} %bitcast.plane_ref, f32[112,8,768]{2,1,0:T(8,128)S(1)} %get-tuple-element.12.carried_ref, f32[128,128]{1,0:T(8,128)S(1)} %bitcast.20, f32[128,128]{1,0:T(8,128)S(1)} %collective-permute-done.f1_ref, ...), custom_call_target="tpu_custom_call" | custom-call | flops 68719476736 | bytes 16777216 | tf_op jit(solution)/shard_map/back_part/pallas_call | solution.py:373
  60.6 0.0 collective-permute-done.5.l3_ref
  60.6 0.0 collective-permute-done.4.l2_ref
  60.6 0.0 copy-start
  60.7 0.0 copy-start.1
  60.7 0.6 finish.1
  61.3 29.0 %all_to_all.11 = f32[64,5,4,128]{3,2,1,0:T(4,128)S(1)} all-to-all(f32[64,5,4,128]{3,2,1,0:T(4,128)S(1)} %bitcast.15), channel_id=1, replica_groups=mesh['ctx'=64,'ch'=4] {'ctx'}, dimensions={0} | all-to-all | bytes 1310720 | tf_op jit(solution)/shard_map/all_to_all | solution.py:426
  90.2 1.0 %unpack.1 = (bf16[256,512]{1,0:T(8,128)(2,1)}, bf16[256,512]{1,0:T(8,128)(2,1)}, f32[256,128]{1,0:T(8,128)}) custom-call(f32[1280,128]{1,0:T(8,128)S(1)} %bitcast.16, bf16[256,512]{1,0:T(8,128)(2,1)S(1)} %copy-done, bf16[256,512]{1,0:T(8,128)(2,1)S(1)} %copy-done.1), custom_call_target="tpu_custom_call" | custom-call | flops 1048576 | bytes 3145728 | tf_op jit(solution)/shard_map/unpack/pallas_call | solution.py:403
  (11 shorter events, 0.0 us)
Async XLA Ops:
  2.3 46.3 %copy-start.2 = (bf16[1536,256]{1,0:T(8,128)(2,1)S(1)}, bf16[1536,256]{1,0:T(8,128)(2,1)}, u32[]{:S(2)}) copy-start(bf16[1536,256]{1,0:T(8,128)(2,1)} %constant.9.clone.inv_ref) | copy-start | bytes 2359300
  2.3 46.3 %copy-start.3 = (bf16[256,512]{1,0:T(8,128)(2,1)S(1)}, bf16[256,512]{1,0:T(8,128)(2,1)}, u32[]{:S(2)}) copy-start(bf16[256,512]{1,0:T(8,128)(2,1)} %g_ref.1) | copy-start | bytes 786436
  2.4 46.3 %copy-start.4 = (bf16[256,512]{1,0:T(8,128)(2,1)S(1)}, bf16[256,512]{1,0:T(8,128)(2,1)}, u32[]{:S(2)}) copy-start(bf16[256,512]{1,0:T(8,128)(2,1)} %c_ref.1) | copy-start | bytes 786436
  2.4 46.3 %copy-start.5 = (s32[8]{0:T(128)S(1)}, s32[8]{0:T(128)}, u32[]{:S(2)}) copy-start(s32[8]{0:T(128)} %genome_ref.3) | copy-start | bytes 100
  2.4 46.3 %copy-start.6 = (bf16[768,512]{1,0:T(8,128)(2,1)S(1)}, bf16[768,512]{1,0:T(8,128)(2,1)}, u32[]{:S(2)}) copy-start(bf16[768,512]{1,0:T(8,128)(2,1)} %constant.8.clone.fwd_ref) | copy-start | bytes 2359300
  46.1 11.2 %collective-permute-start.2 = (f32[128,128]{1,0:T(8,128)S(1)}, f32[128,128]{1,0:T(8,128)S(1)}, u32[]{:S(2)}, u32[]{:S(2)}) collective-permute-start(f32[128,128]{1,0:T(8,128)S(1)} %bitcast.18), channel_id=1, source_target_pairs={{0,3},{1,2},{2,1},{3,0},{4,7},{5,6},{6,5},{7,4},{8,11},{9,10},{10,... | collective-permute-start | bytes 196616 | tf_op jit(solution)/shard_map/ppermute | solution.py:422
  48.7 4.4 %collective-permute-start = (f32[128,128]{1,0:T(8,128)S(1)}, f32[128,128]{1,0:T(8,128)S(1)}, u32[]{:S(2)}, u32[]{:S(2)}) collective-permute-start(f32[128,128]{1,0:T(8,128)S(1)} %bitcast.19), channel_id=1, source_target_pairs={{0,1},{1,0},{2,3},{3,2},{4,5},{5,4},{6,7},{7,6},{8,9},{9,8},{10,11... | collective-permute-start | bytes 196616 | tf_op jit(solution)/shard_map/ppermute | solution.py:422
  53.0 4.4 %collective-permute-start.1 = (f32[128,128]{1,0:T(8,128)S(1)}, f32[128,128]{1,0:T(8,128)S(1)}, u32[]{:S(2)}, u32[]{:S(2)}) collective-permute-start(f32[128,128]{1,0:T(8,128)S(1)} %collective-permute-done.f1_ref), channel_id=1, source_target_pairs={{0,3},{1,2},{2,1},{3,0},{4,7},{5,6},{6,5},{7,4},{8,11},{9,10},{10,... | collective-permute-start | bytes 196616 | tf_op jit(solution)/shard_map/ppermute | solution.py:422
  53.9 6.7 %collective-permute-start.5 = (f32[128,128]{1,0:T(8,128)S(1)}, f32[128,128]{1,0:T(8,128)S(1)}, u32[]{:S(2)}, u32[]{:S(2)}) collective-permute-start(f32[128,128]{1,0:T(8,128)S(1)} %get-tuple-element.20), channel_id=1, source_target_pairs={{0,3},{1,2},{2,1},{3,0},{4,7},{5,6},{6,5},{7,4},{8,11},{9,10},{10,... | collective-permute-start | bytes 196616 | tf_op jit(solution)/shard_map/ppermute | solution.py:422
  55.9 4.7 %collective-permute-start.4 = (f32[128,128]{1,0:T(8,128)S(1)}, f32[128,128]{1,0:T(8,128)S(1)}, u32[]{:S(2)}, u32[]{:S(2)}) collective-permute-start(f32[128,128]{1,0:T(8,128)S(1)} %get-tuple-element.21), channel_id=1, source_target_pairs={{0,2},{1,3},{2,0},{3,1},{4,6},{5,7},{6,4},{7,5},{8,10},{9,11},{10,... | collective-permute-start | bytes 196616 | tf_op jit(solution)/shard_map/ppermute | solution.py:422
  56.6 4.1 %collective-permute-start.3 = (f32[128,128]{1,0:T(8,128)S(1)}, f32[128,128]{1,0:T(8,128)S(1)}, u32[]{:S(2)}, u32[]{:S(2)}) collective-permute-start(f32[128,128]{1,0:T(8,128)S(1)} %get-tuple-element.22), channel_id=1, source_target_pairs={{0,1},{1,0},{2,3},{3,2},{4,5},{5,4},{6,7},{7,6},{8,9},{9,8},{10,11... | collective-permute-start | bytes 196616 | tf_op jit(solution)/shard_map/ppermute | solution.py:422
  60.6 29.6 %copy-start = (bf16[256,512]{1,0:T(8,128)(2,1)S(1)}, bf16[256,512]{1,0:T(8,128)(2,1)}, u32[]{:S(2)}) copy-start(bf16[256,512]{1,0:T(8,128)(2,1)} %q_ref.1) | copy-start | bytes 786436
  60.7 29.6 %copy-start.1 = (bf16[256,512]{1,0:T(8,128)(2,1)S(1)}, bf16[256,512]{1,0:T(8,128)(2,1)}, u32[]{:S(2)}) copy-start(bf16[256,512]{1,0:T(8,128)(2,1)} %k_ref.1) | copy-start | bytes 786436

commit v4 on v3

--- a/solution.py
+++ b/solution.py
@@ -53,7 +53,7 @@
 
 
 def pack_kernel(
-    plane_ref, q_hbm, k_hbm, v_hbm, g_hbm, f_hbm, out_ref, q_ref, k_ref, v_ref, g_ref, f_ref,
+    plane_ref, here_ref, q_hbm, k_hbm, v_hbm, g_hbm, f_hbm, out_ref, q_ref, k_ref, v_ref, g_ref, f_ref,
     turned, sems,
 ):
     column = pl.multiple_of(plane_ref[0] * LANES, LANES)
@@ -62,15 +62,26 @@
         (f_hbm.at[:, pl.ds(column, LANES)], f_ref),
     )
     copies = [pltpu.make_async_copy(a, b, sems.at[i]) for i, (a, b) in enumerate(pairs)]
-    for copy in copies[4:] + copies[:4]:
-        copy.start()
-
-    copies[4].wait()
-    for half in range(2):
-        turned[half, 0:LANES, :] = f_ref[half * LANES : (half + 1) * LANES, :].T
-        for r in range(2):
-            rows = turned[half, pl.ds(r, NCTX, stride=2), :]
-            out_ref[pl.ds(32 + 2 * half + r, NCTX, stride=IN_ROWS), :] = rows
+
+    @pl.when(here_ref[0] < MOST)
+    def _():
+        copies[4].start()
+        for copy in copies[:4]:
+            copy.start()
+        copies[4].wait()
+        for half in range(2):
+            turned[half, 0:LANES, :] = f_ref[half * LANES : (half + 1) * LANES, :].T
+            for r in range(2):
+                rows = turned[half, pl.ds(r, NCTX, stride=2), :]
+                out_ref[pl.ds(32 + 2 * half + r, NCTX, stride=IN_ROWS), :] = rows
+
+    @pl.when(here_ref[0] >= MOST)
+    def _():
+        for copy in copies[:4]:
+            copy.start()
+        for i in range(NCTX):
+            out_ref[IN_ROWS * i + 32 : IN_ROWS * i + 36, :] = jnp.zeros((4, LANES), F32)
+
     for which, (a_ref, b_ref, first_copy) in enumerate(((g_ref, v_ref, 0), (q_ref, k_ref, 2))):
         copies[first_copy].wait()
         copies[first_copy + 1].wait()
@@ -90,8 +101,8 @@
     return (1 - 2 * (lane % 2)).astype(F32)
 
 
-def add_pairs(totals, pairs, first, second):
-    for half in range(2):
+def add_pairs(totals, pairs, first, second, halves=(0, 1), fresh=False):
+    for half in halves:
         loaded = {}
 
         def load(name, view, index):
@@ -106,11 +117,20 @@
             a, b = load("first", first, index), load("second", second, other)
             for i in range(3):
                 lanes = pl.ds(BLOCK * i + LANES * half, LANES)
-                if (j, i) not in out:
+                if (j, i) not in out and not fresh:
                     out[j, i] = totals[j, :, lanes]
-                out[j, i] = out[j, i] + a[i] * b[i]
+                product = a[i] * b[i]
+                out[j, i] = out[j, i] + product if (j, i) in out else product
         for (j, i), value in out.items():
             totals[j, :, pl.ds(BLOCK * i + LANES * half, LANES)] = value
+
+
+def alone(count, function, *args):
+    def body(_, carry):
+        function(*args)
+        return carry
+
+    lax.fori_loop(0, count // MOST, body, 0)
 
 
 def lag_kernel(
@@ -134,27 +154,26 @@
         places.append(s + GAP * own)
     group = 32
     for part in range(NCTX // group):
+        rows = []
         for which in range(2):
-            rows = []
             for s in range(part * group, (part + 1) * group):
                 base = IN_ROWS * s + 16 * which
                 rows.append(
                     jnp.concatenate([x_ref[base : base + 8, :], x_ref[base + 8 : base + 16, :]], 1)
                 )
-            spec = dot3(jnp.concatenate(rows, 0), fwd_ref).reshape(group, OWN, 2 * BLOCK)
-            re, im = spec[:, :, :BLOCK], spec[:, :, BLOCK:]
-            if which == 0:
-                blocks = pl.ds(group * part, group)
-                gated[blocks, :, 0:BLOCK] = re - im
-                gated[blocks, :, BLOCK : 2 * BLOCK] = re
-                gated[blocks, :, 2 * BLOCK : WIDE] = im
-            else:
-                less, more = im - re, re + im
-                for i in range(group):
-                    block = places[part * group + i]
-                    carried_ref[block, :, 0:BLOCK] = re[i]
-                    carried_ref[block, :, BLOCK : 2 * BLOCK] = less[i]
-                    carried_ref[block, :, 2 * BLOCK : WIDE] = more[i]
+        spec = dot3(jnp.concatenate(rows, 0), fwd_ref).reshape(2, group, OWN, 2 * BLOCK)
+        re, im = spec[0, :, :, :BLOCK], spec[0, :, :, BLOCK:]
+        blocks = pl.ds(group * part, group)
+        gated[blocks, :, 0:BLOCK] = re - im
+        gated[blocks, :, BLOCK : 2 * BLOCK] = re
+        gated[blocks, :, 2 * BLOCK : WIDE] = im
+        re, im = spec[1, :, :, :BLOCK], spec[1, :, :, BLOCK:]
+        less, more = im - re, re + im
+        for i in range(group):
+            block = places[part * group + i]
+            carried_ref[block, :, 0:BLOCK] = re[i]
+            carried_ref[block, :, BLOCK : 2 * BLOCK] = less[i]
+            carried_ref[block, :, 2 * BLOCK : WIDE] = more[i]
     pairs = [(j, u, u + j) for u in range(UNROLL) for j in range(TILE)]
 
     def genome(g, begin):
@@ -230,6 +249,20 @@
         count = genome_ref[g]
         first = begin + GAP * g
 
+        @pl.when(count == MOST)
+        def _():
+            taps, later = filt.at[head : head + MOST], carried_ref.at[pl.ds(first, MOST)]
+            for b in range(0, MOST, TILE):
+                every = [
+                    (j, t - b - j, t)
+                    for t in range(b, MOST)
+                    for j in range(TILE)
+                    if t >= b + j
+                ]
+                rows = back.at[pl.ds(begin + b, TILE)]
+                for half in range(2):
+                    alone(count, add_pairs, rows, every, taps, later, (half,), True)
+
         def tile(i, _):
             b = TILE * i
 
@@ -246,7 +279,8 @@
             lax.fori_loop(0, (count - b + UNROLL - 1) // UNROLL, step, 0)
             return 0
 
-        lax.fori_loop(0, (count + TILE - 1) // TILE, tile, 0)
+        tiles = jnp.where(count == MOST, 0, (count + TILE - 1) // TILE)
+        lax.fori_loop(0, tiles, tile, 0)
         return begin + count
 
     lax.fori_loop(0, GENOMES, genome, jnp.int32(0))
@@ -327,12 +361,12 @@
     return [pltpu.with_memory_space_constraint(a, pltpu.HBM) for a in arrays]
 
 
-def pack(plane, q, k, v, g, f):
+def pack(plane, here, q, k, v, g, f):
     half = pltpu.VMEM(q.shape, BF16)
     return pl.pallas_call(
         pack_kernel,
         out_shape=pltpu.VMEM((NCTX * IN_ROWS, LANES), F32),
-        in_specs=[SMEM] + [HBM] * 5,
+        in_specs=[SMEM] * 2 + [HBM] * 5,
         out_specs=VMEM,
         scratch_shapes=[half] * 4
         + [
@@ -343,7 +377,7 @@
         compiler_params=params(),
         cost_estimate=cost(1 << 20, 3 << 20),
         name="pack",
-    )(plane, *in_hbm(q, k, v, g, f))
+    )(plane, here, *in_hbm(q, k, v, g, f))
 
 
 def lag_part(genome_blocks, plane, x, tables, g, c):
@@ -429,15 +463,16 @@
 def local(q, k, v, g, c, filters, genome_blocks):
     forward, inverse = [jnp.asarray(t) for t in dft_tables()]
     plane = lax.axis_index("ch").astype(jnp.int32).reshape(1)
-    sent = pack(plane, q, k, v, g, filters)
+    here = lax.axis_index("ctx").astype(jnp.int32).reshape(1)
+    sent = pack(plane, here, q, k, v, g, filters)
     got = exchange(sent.reshape(NCTX, IN_ROWS // 4, 4, LANES))
     own_quarter = got[:MOST, 8].reshape(4 * MOST, LANES)
     near, other = shift(own_quarter, 1), shift(own_quarter, 3)
     slots, carried, grad_value = lag_part(
         genome_blocks, plane, got.reshape(NCTX * IN_ROWS, LANES), (forward, inverse), g, c
     )
-    slots, relayed = lax.optimization_barrier((slots, near))
-    quarters = [own_quarter, near, shift(relayed, 3), other]
+    slots, relayed = lax.optimization_barrier((slots, other))
+    quarters = [own_quarter, near, shift(relayed, 1), other]
     lags = [slots[0]] + [shift(slots[i], i) for i in range(1, PLANES)]
     back = back_part(genome_blocks, plane, carried, quarters, forward)
     out = finish(back, lags, inverse).reshape(NCTX, OUT_ROWS // 4, 4, LANES)

time: 91.4 us -> 91.3 us (level)
  transfers between devices with their start and end apart: 6 -> 6, of which waited for: 1 -> 0; matrix products, arithmetic and copies ran while one was open for 0% -> 0% of each run, Pallas kernels for 8% -> 8%
where the time goes in v4:
time: 91.3 us
  blocking collectives  72.1 us (79%)
  Pallas kernels  10.9 us (12%)
  starting transfers between devices  7.43 us (8%)
    all_to_all x2, blocking collectives, exchange(): return lax.all_to_all(x, 'ctx', split_axis=0, concat_axis=0, tiled=True)  72.1 us
    ppermute x6, starting transfers between devices, shift(): return lax.ppermute(x, 'ch', [(i, i ^ k) for i in range(PLANES)])  7.43 us
    pallas_call x1, Pallas kernels, lag_part(): pl.pallas_call(lag_kernel, out_shape=[shape(PLANES, 4 * MOST, LANES), sha...  4.48 us
    pallas_call x1, Pallas kernels, back_part(): pl.pallas_call(back_kernel, out_shape=shape(NCTX + TILE, OWN, WIDE), in_s...  3.07 us
  transfers between devices with their start and end apart: 6, of which 0 were waited for; matrix products, arithmetic and copies ran while one was open for 0% of the time, Pallas kernels for 8%

profile of v4, /device:TPU:1, one launch (start us, length us, event | category | flops | bytes accessed | tf_op | source)
XLA Modules:
  0.0 91.3 jit_solution(2409163263530749958)
XLA Ops:
  0.6 1.7 %pack.1 = f32[2304,128]{1,0:T(8,128)S(1)} custom-call(s32[1]{0:T(128)} %bitcast.plane_ref, s32[1]{0:T(128)} %bitcast.1.here_ref, bf16[256,512]{1,0:T(8,128)(2,1)} %q_ref.1, bf16[256,512]{1,0:T(8,128)(2,1)} %k_ref.1, bf16[256,512]{1,0:T(8,128)(2,1)} %v_hbm.1, bf16[256,512]{1,0:T(8,128)(2,1)} %g_ref.1, f32[256,512]{1,0:T(8,128)} %f_hbm.1), custom_call_target="tpu_custom_call" | custom-call | flops 1048576 | bytes 3145728 | tf_op jit(solution)/shard_map/pack/pallas_call | solution.py:366
  2.3 0.0 copy-start.2
  2.3 0.0 copy-start.3
  2.4 0.0 copy-start.4
  2.4 0.0 copy-start.5
  2.4 0.0 copy-start.6
  2.4 43.6 %all_to_all.10 = f32[64,9,4,128]{3,2,1,0:T(4,128)S(1)} all-to-all(f32[64,9,4,128]{3,2,1,0:T(4,128)S(1)} %bitcast.15), channel_id=1, replica_groups=mesh['ctx'=64,'ch'=4] {'ctx'}, dimensions={0} | all-to-all | bytes 2359296 | tf_op jit(solution)/shard_map/all_to_all | solution.py:460
  46.0 2.6 %collective-permute-start.1 = (f32[128,128]{1,0:T(8,128)S(1)}, f32[128,128]{1,0:T(8,128)S(1)}, u32[]{:S(2)}, u32[]{:S(2)}) collective-permute-start(f32[128,128]{1,0:T(8,128)S(1)} %bitcast.19), channel_id=1, source_target_pairs={{0,3},{1,2},{2,1},{3,0},{4,7},{5,6},{6,5},{7,4},{8,11},{9,10},{10,... | collective-permute-start | bytes 196616 | tf_op jit(solution)/shard_map/ppermute | solution.py:456
  48.6 0.0 collective-permute-start
  48.6 4.5 %lag_part.1 = (f32[4,128,128]{2,1,0:T(8,128)S(1)}, f32[112,8,768]{2,1,0:T(8,128)S(1)}, bf16[256,512]{1,0:T(8,128)(2,1)}) custom-call(s32[8]{0:T(128)S(1)} %copy-done.5, s32[1]{0:T(128)} %bitcast.plane_ref, f32[2304,128]{1,0:T(8,128)S(1)} %bitcast.18, bf16[768,512]{1,0:T(8,128)(2,1)S(1)} %copy-done.6, bf16[1536,256]{1,0:T(8,128)(2,1)S(1)} %copy-done.2, ...), custom_call_target="tpu_custom_call" | custom-call | flops 68719476736 | bytes 16777216 | tf_op jit(solution)/shard_map/lag_part/pallas_call | solution.py:384
  53.1 0.0 collective-permute-done.1.f3_ref
  53.1 1.5 %collective-permute-start.2 = (f32[128,128]{1,0:T(8,128)S(1)}, f32[128,128]{1,0:T(8,128)S(1)}, u32[]{:S(2)}, u32[]{:S(2)}) collective-permute-start(f32[128,128]{1,0:T(8,128)S(1)} %collective-permute-done.1.f3_ref), channel_id=1, source_target_pairs={{0,1},{1,0},{2,3},{3,2},{4,5},{5,4},{6,7},{7,6},{8,9},{9,8},{10,11... | collective-permute-start | bytes 196616 | tf_op jit(solution)/shard_map/ppermute | solution.py:456
  54.7 0.3 collective-permute-start.5
  55.0 1.6 %collective-permute-start.4 = (f32[128,128]{1,0:T(8,128)S(1)}, f32[128,128]{1,0:T(8,128)S(1)}, u32[]{:S(2)}, u32[]{:S(2)}) collective-permute-start(f32[128,128]{1,0:T(8,128)S(1)} %get-tuple-element.21), channel_id=1, source_target_pairs={{0,2},{1,3},{2,0},{3,1},{4,6},{5,7},{6,4},{7,5},{8,10},{9,11},{10,... | collective-permute-start | bytes 196616 | tf_op jit(solution)/shard_map/ppermute | solution.py:456
  56.6 1.4 %collective-permute-start.3 = (f32[128,128]{1,0:T(8,128)S(1)}, f32[128,128]{1,0:T(8,128)S(1)}, u32[]{:S(2)}, u32[]{:S(2)}) collective-permute-start(f32[128,128]{1,0:T(8,128)S(1)} %get-tuple-element.22), channel_id=1, source_target_pairs={{0,1},{1,0},{2,3},{3,2},{4,5},{5,4},{6,7},{7,6},{8,9},{9,8},{10,11... | collective-permute-start | bytes 196616 | tf_op jit(solution)/shard_map/ppermute | solution.py:456
  58.0 0.0 collective-permute-done.2.f2_ref
  58.0 3.1 %back_part.1.back = f32[68,8,768]{2,1,0:T(8,128)S(1)} custom-call(s32[8]{0:T(128)S(1)} %copy-done.5, s32[1]{0:T(128)} %bitcast.plane_ref, f32[112,8,768]{2,1,0:T(8,128)S(1)} %get-tuple-element.12.carried_ref, f32[128,128]{1,0:T(8,128)S(1)} %bitcast.21, f32[128,128]{1,0:T(8,128)S(1)} %collective-permute-done.f1_ref, ...), custom_call_target="tpu_custom_call" | custom-call | flops 68719476736 | bytes 16777216 | tf_op jit(solution)/shard_map/back_part/pallas_call | solution.py:407
  61.1 0.0 collective-permute-done.4.l2_ref
  61.1 0.0 collective-permute-done.3.l1_ref
  61.1 0.0 copy-start
  61.1 0.0 copy-start.1
  61.2 0.6 finish.1
  61.8 28.5 %all_to_all.11 = f32[64,5,4,128]{3,2,1,0:T(4,128)S(1)} all-to-all(f32[64,5,4,128]{3,2,1,0:T(4,128)S(1)} %bitcast.16), channel_id=1, replica_groups=mesh['ctx'=64,'ch'=4] {'ctx'}, dimensions={0} | all-to-all | bytes 1310720 | tf_op jit(solution)/shard_map/all_to_all | solution.py:460
  90.2 1.0 %unpack.1 = (bf16[256,512]{1,0:T(8,128)(2,1)}, bf16[256,512]{1,0:T(8,128)(2,1)}, f32[256,128]{1,0:T(8,128)}) custom-call(f32[1280,128]{1,0:T(8,128)S(1)} %bitcast.17, bf16[256,512]{1,0:T(8,128)(2,1)S(1)} %copy-done, bf16[256,512]{1,0:T(8,128)(2,1)S(1)} %copy-done.1), custom_call_target="tpu_custom_call" | custom-call | flops 1048576 | bytes 3145728 | tf_op jit(solution)/shard_map/unpack/pallas_call | solution.py:437
  (11 shorter events, 0.1 us)
Async XLA Ops:
  2.3 46.3 %copy-start.2 = (bf16[1536,256]{1,0:T(8,128)(2,1)S(1)}, bf16[1536,256]{1,0:T(8,128)(2,1)}, u32[]{:S(2)}) copy-start(bf16[1536,256]{1,0:T(8,128)(2,1)} %constant.14.clone.inv_ref) | copy-start | bytes 2359300
  2.3 46.3 %copy-start.3 = (bf16[256,512]{1,0:T(8,128)(2,1)S(1)}, bf16[256,512]{1,0:T(8,128)(2,1)}, u32[]{:S(2)}) copy-start(bf16[256,512]{1,0:T(8,128)(2,1)} %g_ref.1) | copy-start | bytes 786436
  2.4 46.2 %copy-start.4 = (bf16[256,512]{1,0:T(8,128)(2,1)S(1)}, bf16[256,512]{1,0:T(8,128)(2,1)}, u32[]{:S(2)}) copy-start(bf16[256,512]{1,0:T(8,128)(2,1)} %c_ref.1) | copy-start | bytes 786436
  2.4 46.2 %copy-start.5 = (s32[8]{0:T(128)S(1)}, s32[8]{0:T(128)}, u32[]{:S(2)}) copy-start(s32[8]{0:T(128)} %genome_ref.3) | copy-start | bytes 100
  2.4 46.2 %copy-start.6 = (bf16[768,512]{1,0:T(8,128)(2,1)S(1)}, bf16[768,512]{1,0:T(8,128)(2,1)}, u32[]{:S(2)}) copy-start(bf16[768,512]{1,0:T(8,128)(2,1)} %constant.13.clone.fwd_ref) | copy-start | bytes 2359300
  46.0 7.1 %collective-permute-start.1 = (f32[128,128]{1,0:T(8,128)S(1)}, f32[128,128]{1,0:T(8,128)S(1)}, u32[]{:S(2)}, u32[]{:S(2)}) collective-permute-start(f32[128,128]{1,0:T(8,128)S(1)} %bitcast.19), channel_id=1, source_target_pairs={{0,3},{1,2},{2,1},{3,0},{4,7},{5,6},{6,5},{7,4},{8,11},{9,10},{10,... | collective-permute-start | bytes 196616 | tf_op jit(solution)/shard_map/ppermute | solution.py:456
  48.6 9.4 %collective-permute-start = (f32[128,128]{1,0:T(8,128)S(1)}, f32[128,128]{1,0:T(8,128)S(1)}, u32[]{:S(2)}, u32[]{:S(2)}) collective-permute-start(f32[128,128]{1,0:T(8,128)S(1)} %bitcast.20), channel_id=1, source_target_pairs={{0,1},{1,0},{2,3},{3,2},{4,5},{5,4},{6,7},{7,6},{8,9},{9,8},{10,11... | collective-permute-start | bytes 196616 | tf_op jit(solution)/shard_map/ppermute | solution.py:456
  53.1 4.9 %collective-permute-start.2 = (f32[128,128]{1,0:T(8,128)S(1)}, f32[128,128]{1,0:T(8,128)S(1)}, u32[]{:S(2)}, u32[]{:S(2)}) collective-permute-start(f32[128,128]{1,0:T(8,128)S(1)} %collective-permute-done.1.f3_ref), channel_id=1, source_target_pairs={{0,1},{1,0},{2,3},{3,2},{4,5},{5,4},{6,7},{7,6},{8,9},{9,8},{10,11... | collective-permute-start | bytes 196616 | tf_op jit(solution)/shard_map/ppermute | solution.py:456
  54.7 6.4 %collective-permute-start.5 = (f32[128,128]{1,0:T(8,128)S(1)}, f32[128,128]{1,0:T(8,128)S(1)}, u32[]{:S(2)}, u32[]{:S(2)}) collective-permute-start(f32[128,128]{1,0:T(8,128)S(1)} %get-tuple-element.20), channel_id=1, source_target_pairs={{0,3},{1,2},{2,1},{3,0},{4,7},{5,6},{6,5},{7,4},{8,11},{9,10},{10,... | collective-permute-start | bytes 196616 | tf_op jit(solution)/shard_map/ppermute | solution.py:456
  55.0 6.2 %collective-permute-start.4 = (f32[128,128]{1,0:T(8,128)S(1)}, f32[128,128]{1,0:T(8,128)S(1)}, u32[]{:S(2)}, u32[]{:S(2)}) collective-permute-start(f32[128,128]{1,0:T(8,128)S(1)} %get-tuple-element.21), channel_id=1, source_target_pairs={{0,2},{1,3},{2,0},{3,1},{4,6},{5,7},{6,4},{7,5},{8,10},{9,11},{10,... | collective-permute-start | bytes 196616 | tf_op jit(solution)/shard_map/ppermute | solution.py:456
  56.6 4.5 %collective-permute-start.3 = (f32[128,128]{1,0:T(8,128)S(1)}, f32[128,128]{1,0:T(8,128)S(1)}, u32[]{:S(2)}, u32[]{:S(2)}) collective-permute-start(f32[128,128]{1,0:T(8,128)S(1)} %get-tuple-element.22), channel_id=1, source_target_pairs={{0,1},{1,0},{2,3},{3,2},{4,5},{5,4},{6,7},{7,6},{8,9},{9,8},{10,11... | collective-permute-start | bytes 196616 | tf_op jit(solution)/shard_map/ppermute | solution.py:456
  61.1 29.1 %copy-start = (bf16[256,512]{1,0:T(8,128)(2,1)S(1)}, bf16[256,512]{1,0:T(8,128)(2,1)}, u32[]{:S(2)}) copy-start(bf16[256,512]{1,0:T(8,128)(2,1)} %q_ref.1) | copy-start | bytes 786436
  61.1 29.1 %copy-start.1 = (bf16[256,512]{1,0:T(8,128)(2,1)S(1)}, bf16[256,512]{1,0:T(8,128)(2,1)}, u32[]{:S(2)}) copy-start(bf16[256,512]{1,0:T(8,128)(2,1)} %k_ref.1) | copy-start | bytes 786436

commit v5 on v4

--- a/solution.py
+++ b/solution.py
@@ -225,13 +225,14 @@
 
 
 def back_kernel(
-    genome_ref, plane_ref, carried_ref, f0_ref, f1_ref, f2_ref, f3_ref, fwd_ref, back, filt, flat,
+    genome_ref, plane_ref, carried_ref, own_ref, near_ref, both_ref, fwd_ref, back, filt, flat,
 ):
-    for k, f_ref in enumerate((f0_ref, f1_ref, f2_ref, f3_ref)):
+    sources = ((own_ref, 0), (both_ref, 0), (both_ref, 4 * MOST), (near_ref, 0))
+    for k, (f_ref, top) in enumerate(sources):
         quarter = lax.bitwise_xor(jnp.int32(k), plane_ref[0])
         for half in range(2):
             for r in range(2):
-                rows = f_ref[pl.ds(2 * half + r, MOST, stride=4), :]
+                rows = f_ref[pl.ds(top + 2 * half + r, MOST, stride=4), :]
                 flat[half, pl.ds(2 * quarter + r, MOST, stride=OWN), :] = rows
     spec = dot3(jnp.concatenate([flat[0], flat[1]], 1), fwd_ref)
     sign = signs()
@@ -403,11 +404,11 @@
     )(genome_blocks, plane, x, *tables, g, c)
 
 
-def back_part(genome_blocks, plane, carried, quarters, table):
+def back_part(genome_blocks, plane, carried, own, near, both, table):
     return pl.pallas_call(
         back_kernel,
         out_shape=shape(NCTX + TILE, OWN, WIDE),
-        in_specs=[SMEM, SMEM] + [VMEM] * 6,
+        in_specs=[SMEM, SMEM] + [VMEM] * 5,
         out_specs=VMEM,
         scratch_shapes=[
             pltpu.VMEM((TILE - 1 + MOST + UNROLL, OWN, WIDE), F32),
@@ -416,7 +417,7 @@
         compiler_params=params(),
         cost_estimate=cost(1 << 36, 16 << 20),
         name="back_part",
-    )(genome_blocks, plane, carried, *quarters, table)
+    )(genome_blocks, plane, carried, own, near, both, table)
 
 
 def finish(back, lags, table):
@@ -467,14 +468,14 @@
     sent = pack(plane, here, q, k, v, g, filters)
     got = exchange(sent.reshape(NCTX, IN_ROWS // 4, 4, LANES))
     own_quarter = got[:MOST, 8].reshape(4 * MOST, LANES)
-    near, other = shift(own_quarter, 1), shift(own_quarter, 3)
+    near = shift(own_quarter, 3)
     slots, carried, grad_value = lag_part(
         genome_blocks, plane, got.reshape(NCTX * IN_ROWS, LANES), (forward, inverse), g, c
     )
-    slots, relayed = lax.optimization_barrier((slots, other))
-    quarters = [own_quarter, near, shift(relayed, 1), other]
+    slots, near = lax.optimization_barrier((slots, near))
+    both = shift(jnp.concatenate([own_quarter, near], axis=0), 1)
     lags = [slots[0]] + [shift(slots[i], i) for i in range(1, PLANES)]
-    back = back_part(genome_blocks, plane, carried, quarters, forward)
+    back = back_part(genome_blocks, plane, carried, own_quarter, near, both, forward)
     out = finish(back, lags, inverse).reshape(NCTX, OUT_ROWS // 4, 4, LANES)
     returned = exchange(out).reshape(NCTX * OUT_ROWS, LANES)
     scale = (NCTX * BLOCK) ** (-0.5)

time: 91.3 us -> 91.4 us (level)
  starting transfers between devices: 7.43 us -> 6 us
  waiting for transfers between devices: 0.02 us -> 1 us
    ppermute x6 -> x5, starting transfers between devices: 7.43 us -> 6 us  [shift(): return lax.ppermute(x, 'ch', [(i, i ^ k) for i in range(PLANES)])]
    ppermute x6 -> x5, waiting for transfers between devices: 0.02 us -> 1 us  [shift(): return lax.ppermute(x, 'ch', [(i, i ^ k) for i in range(PLANES)])]
  transfers between devices with their start and end apart: 6 -> 5, of which waited for: 0 -> 2; matrix products, arithmetic and copies ran while one was open for 0% -> 0% of each run, Pallas kernels for 8% -> 8%
where the time goes in v5:
time: 91.4 us; the launch traced here: 91.1 us
  blocking collectives  72.5 us (79%)
  Pallas kernels  10.7 us (12%)
  starting transfers between devices  6 us (7%)
  waiting for transfers between devices  1 us (1%)
    all_to_all x2, blocking collectives, exchange(): return lax.all_to_all(x, 'ctx', split_axis=0, concat_axis=0, tiled=True)  72.5 us
    ppermute x5, starting transfers between devices, shift(): return lax.ppermute(x, 'ch', [(i, i ^ k) for i in range(PLANES)])  6 us
    pallas_call x1, Pallas kernels, lag_part(): pl.pallas_call(lag_kernel, out_shape=[shape(PLANES, 4 * MOST, LANES), sha...  4.4 us
    pallas_call x1, Pallas kernels, back_part(): pl.pallas_call(back_kernel, out_shape=shape(NCTX + TILE, OWN, WIDE), in_s...  2.98 us
  transfers between devices with their start and end apart: 5, of which 2 were waited for; matrix products, arithmetic and copies ran while one was open for 0% of the time, Pallas kernels for 8%

profile of v5, /device:TPU:1, one launch (start us, length us, event | category | flops | bytes accessed | tf_op | source)
XLA Modules:
  0.0 91.1 jit_solution(12741772463045556016)
XLA Ops:
  0.6 1.7 %pack.1 = f32[2304,128]{1,0:T(8,128)S(1)} custom-call(s32[1]{0:T(128)} %bitcast.plane_ref, s32[1]{0:T(128)} %bitcast.1.here_ref, bf16[256,512]{1,0:T(8,128)(2,1)} %q_ref.1, bf16[256,512]{1,0:T(8,128)(2,1)} %k_ref.1, bf16[256,512]{1,0:T(8,128)(2,1)} %v_hbm.1, bf16[256,512]{1,0:T(8,128)(2,1)} %g_ref.1, f32[256,512]{1,0:T(8,128)} %f_hbm.1), custom_call_target="tpu_custom_call" | custom-call | flops 1048576 | bytes 3145728 | tf_op jit(solution)/shard_map/pack/pallas_call | solution.py:367
  2.3 0.0 copy-start.2
  2.3 0.0 copy-start.3
  2.4 0.0 copy-start.4
  2.4 0.0 copy-start.5
  2.4 0.0 copy-start.6
  2.4 43.6 %all_to_all.10 = f32[64,9,4,128]{3,2,1,0:T(4,128)S(1)} all-to-all(f32[64,9,4,128]{3,2,1,0:T(4,128)S(1)} %bitcast.15), channel_id=1, replica_groups=mesh['ctx'=64,'ch'=4] {'ctx'}, dimensions={0} | all-to-all | bytes 2359296 | tf_op jit(solution)/shard_map/all_to_all | solution.py:461
  46.0 2.6 %collective-permute-start = (f32[128,128]{1,0:T(8,128)S(1)}, f32[128,128]{1,0:T(8,128)S(1)}, u32[]{:S(2)}, u32[]{:S(2)}) collective-permute-start(f32[128,128]{1,0:T(8,128)S(1)} %bitcast.19), channel_id=1, source_target_pairs={{0,3},{1,2},{2,1},{3,0},{4,7},{5,6},{6,5},{7,4},{8,11},{9,10},{10,... | collective-permute-start | bytes 196616 | tf_op jit(solution)/shard_map/ppermute | solution.py:457
  48.6 0.0 copy-done.2
  48.6 0.0 copy-done.6
  48.6 4.4 %lag_part.1 = (f32[4,128,128]{2,1,0:T(8,128)S(1)}, f32[112,8,768]{2,1,0:T(8,128)S(1)}, bf16[256,512]{1,0:T(8,128)(2,1)}) custom-call(s32[8]{0:T(128)S(1)} %copy-done.5, s32[1]{0:T(128)} %bitcast.plane_ref, f32[2304,128]{1,0:T(8,128)S(1)} %bitcast.18, bf16[768,512]{1,0:T(8,128)(2,1)S(1)} %copy-done.6, bf16[1536,256]{1,0:T(8,128)(2,1)S(1)} %copy-done.2, ...), custom_call_target="tpu_custom_call" | custom-call | flops 68719476736 | bytes 16777216 | tf_op jit(solution)/shard_map/lag_part/pallas_call | solution.py:385
  53.0 0.0 collective-permute-done.near_ref
  53.1 0.1 collective-permute-start.1
  53.2 0.9 collective-permute-start.4
  54.0 2.5 %collective-permute-start.3 = (f32[128,128]{1,0:T(8,128)S(1)}, f32[128,128]{1,0:T(8,128)S(1)}, u32[]{:S(2)}, u32[]{:S(2)}) collective-permute-start(f32[128,128]{1,0:T(8,128)S(1)} %get-tuple-element.21), channel_id=1, source_target_pairs={{0,2},{1,3},{2,0},{3,1},{4,6},{5,7},{6,4},{7,5},{8,10},{9,11},{10,... | collective-permute-start | bytes 196616 | tf_op jit(solution)/shard_map/ppermute | solution.py:457
  56.5 0.0 collective-permute-start.2
  56.5 0.4 collective-permute-done.1.both_ref
  57.0 3.0 %back_part.1.back = f32[68,8,768]{2,1,0:T(8,128)S(1)} custom-call(s32[8]{0:T(128)S(1)} %copy-done.5, s32[1]{0:T(128)} %bitcast.plane_ref, f32[112,8,768]{2,1,0:T(8,128)S(1)} %get-tuple-element.12.carried_ref, f32[128,128]{1,0:T(8,128)S(1)} %bitcast.21, f32[128,128]{1,0:T(8,128)S(1)} %collective-permute-done.near_ref, ...), custom_call_target="tpu_custom_call" | custom-call | flops 68719476736 | bytes 16777216 | tf_op jit(solution)/shard_map/back_part/pallas_call | solution.py:408
  59.9 0.0 collective-permute-done.4.l3_ref
  60.0 0.0 collective-permute-done.3.l2_ref
  60.0 0.6 collective-permute-done.2.l1_ref
  60.5 0.6 finish.1
  61.1 28.9 %all_to_all.11 = f32[64,5,4,128]{3,2,1,0:T(4,128)S(1)} all-to-all(f32[64,5,4,128]{3,2,1,0:T(4,128)S(1)} %bitcast.16), channel_id=1, replica_groups=mesh['ctx'=64,'ch'=4] {'ctx'}, dimensions={0} | all-to-all | bytes 1310720 | tf_op jit(solution)/shard_map/all_to_all | solution.py:461
  90.0 1.0 %unpack.1 = (bf16[256,512]{1,0:T(8,128)(2,1)}, bf16[256,512]{1,0:T(8,128)(2,1)}, f32[256,128]{1,0:T(8,128)}) custom-call(f32[1280,128]{1,0:T(8,128)S(1)} %bitcast.17, bf16[256,512]{1,0:T(8,128)(2,1)S(1)} %copy-done, bf16[256,512]{1,0:T(8,128)(2,1)S(1)} %copy-done.1), custom_call_target="tpu_custom_call" | custom-call | flops 1048576 | bytes 3145728 | tf_op jit(solution)/shard_map/unpack/pallas_call | solution.py:438
  (10 shorter events, 0.1 us)
Async XLA Ops:
  2.3 46.3 %copy-start.2 = (bf16[1536,256]{1,0:T(8,128)(2,1)S(1)}, bf16[1536,256]{1,0:T(8,128)(2,1)}, u32[]{:S(2)}) copy-start(bf16[1536,256]{1,0:T(8,128)(2,1)} %constant.14.clone.inv_ref) | copy-start | bytes 2359300
  2.3 46.3 %copy-start.3 = (bf16[256,512]{1,0:T(8,128)(2,1)S(1)}, bf16[256,512]{1,0:T(8,128)(2,1)}, u32[]{:S(2)}) copy-start(bf16[256,512]{1,0:T(8,128)(2,1)} %g_ref.1) | copy-start | bytes 786436
  2.4 46.2 %copy-start.4 = (bf16[256,512]{1,0:T(8,128)(2,1)S(1)}, bf16[256,512]{1,0:T(8,128)(2,1)}, u32[]{:S(2)}) copy-start(bf16[256,512]{1,0:T(8,128)(2,1)} %c_ref.1) | copy-start | bytes 786436
  2.4 46.2 %copy-start.5 = (s32[8]{0:T(128)S(1)}, s32[8]{0:T(128)}, u32[]{:S(2)}) copy-start(s32[8]{0:T(128)} %genome_ref.3) | copy-start | bytes 100
  2.4 46.2 %copy-start.6 = (bf16[768,512]{1,0:T(8,128)(2,1)S(1)}, bf16[768,512]{1,0:T(8,128)(2,1)}, u32[]{:S(2)}) copy-start(bf16[768,512]{1,0:T(8,128)(2,1)} %constant.13.clone.fwd_ref) | copy-start | bytes 2359300
  46.0 7.0 %collective-permute-start = (f32[128,128]{1,0:T(8,128)S(1)}, f32[128,128]{1,0:T(8,128)S(1)}, u32[]{:S(2)}, u32[]{:S(2)}) collective-permute-start(f32[128,128]{1,0:T(8,128)S(1)} %bitcast.19), channel_id=1, source_target_pairs={{0,3},{1,2},{2,1},{3,0},{4,7},{5,6},{6,5},{7,4},{8,11},{9,10},{10,... | collective-permute-start | bytes 196616 | tf_op jit(solution)/shard_map/ppermute | solution.py:457
  53.1 3.9 %collective-permute-start.1 = (f32[256,128]{1,0:T(8,128)S(1)}, f32[256,128]{1,0:T(8,128)S(1)}, u32[]{:S(2)}, u32[]{:S(2)}) collective-permute-start(f32[256,128]{1,0:T(8,128)S(1)} %pad_maximum_fusion), channel_id=1, source_target_pairs={{0,1},{1,0},{2,3},{3,2},{4,5},{5,4},{6,7},{7,6},{8,9},{9,8},{10,11... | collective-permute-start | bytes 393224 | tf_op jit(solution)/shard_map/ppermute | solution.py:457
  53.2 6.8 %collective-permute-start.4 = (f32[128,128]{1,0:T(8,128)S(1)}, f32[128,128]{1,0:T(8,128)S(1)}, u32[]{:S(2)}, u32[]{:S(2)}) collective-permute-start(f32[128,128]{1,0:T(8,128)S(1)} %get-tuple-element.20), channel_id=1, source_target_pairs={{0,3},{1,2},{2,1},{3,0},{4,7},{5,6},{6,5},{7,4},{8,11},{9,10},{10,... | collective-permute-start | bytes 196616 | tf_op jit(solution)/shard_map/ppermute | solution.py:457
  54.0 5.9 %collective-permute-start.3 = (f32[128,128]{1,0:T(8,128)S(1)}, f32[128,128]{1,0:T(8,128)S(1)}, u32[]{:S(2)}, u32[]{:S(2)}) collective-permute-start(f32[128,128]{1,0:T(8,128)S(1)} %get-tuple-element.21), channel_id=1, source_target_pairs={{0,2},{1,3},{2,0},{3,1},{4,6},{5,7},{6,4},{7,5},{8,10},{9,11},{10,... | collective-permute-start | bytes 196616 | tf_op jit(solution)/shard_map/ppermute | solution.py:457
  56.5 4.0 %collective-permute-start.2 = (f32[128,128]{1,0:T(8,128)S(1)}, f32[128,128]{1,0:T(8,128)S(1)}, u32[]{:S(2)}, u32[]{:S(2)}) collective-permute-start(f32[128,128]{1,0:T(8,128)S(1)} %get-tuple-element.22), channel_id=1, source_target_pairs={{0,1},{1,0},{2,3},{3,2},{4,5},{5,4},{6,7},{7,6},{8,9},{9,8},{10,11... | collective-permute-start | bytes 196616 | tf_op jit(solution)/shard_map/ppermute | solution.py:457
  60.5 29.5 %copy-start = (bf16[256,512]{1,0:T(8,128)(2,1)S(1)}, bf16[256,512]{1,0:T(8,128)(2,1)}, u32[]{:S(2)}) copy-start(bf16[256,512]{1,0:T(8,128)(2,1)} %q_ref.1) | copy-start | bytes 786436
  60.5 29.5 %copy-start.1 = (bf16[256,512]{1,0:T(8,128)(2,1)S(1)}, bf16[256,512]{1,0:T(8,128)(2,1)}, u32[]{:S(2)}) copy-start(bf16[256,512]{1,0:T(8,128)(2,1)} %k_ref.1) | copy-start | bytes 786436
